TPU v7x, 256 devices: a whole 4x4x8 slice. The times are simulated.
256 devices in a mesh: layer: 2 (over x_lo), wide: 16 (over z, x_hi), tp: 8 (over y, core).
Axes of the slice: x: 4 (x_hi: 2, x_lo: 2; x = x_hi * 2 + x_lo), y: 4, z: 8, core: 2. Of those that a mesh axis runs over, the one named last changes fastest.
Arguments:
- activations: bfloat16 [2048, 28672], P(('layer', 'wide'), 'tp'), parts along dimension 0, may hold values from -6 to 6
- grads_out: bfloat16 [16384, 1024], P(('layer', 'wide'), 'tp'), parts along dimension 0, may hold values from -6 to 6
- basis_in: bfloat16 [57344, 14336], P(('layer', 'tp'), 'wide'), parts along dimension 0, may hold values from -0.03125 to 0.03125
- basis_out: bfloat16 [16384, 8192], P(('layer', 'wide'), 'tp'), parts along dimension 0, may hold values from -0.0625 to 0.0625
- lengths: int32 [8], replicated, may hold values from 32 to 128, as said below
Outputs:
- eigenvalues: float32 [16384, 14336], P(('layer', 'tp'), 'wide'), parts along dimension 0
There are 2 independent parts, one for each index of `layer`. A program takes and returns all parts, laid end to end along the dimension named above; an argument that names none is the same for every part. Nothing has to cross between parts.
Inputs may be any that keep to these rules, and one draw needn't show every extreme that they name: `lengths`: every draw has a sequence with all 128 tokens live.
All inputs are finite; a program needn't handle non-finite values.
Results may differ from a plain program's by a relative error of at most 0.0029.
Values may be sent and summed in bfloat16 or wider, within the bound.
No kernel may reach another device: no remote copies, remote signals or barrier semaphores. Data moves between devices by JAX's collectives and lax.ppermute only.
A program may use at most 64 MiB of HBM per device.

v0:
```python
import jax
import jax.numpy as jnp
from jax import lax
from jax.sharding import PartitionSpec as P

LEN = 128
SEQS = 8


def on_device(activations, grads_out, basis_in, basis_out, lengths):
    local_tokens = grads_out.shape[1]
    token_index = lax.axis_index("tp") * local_tokens + lax.iota(jnp.int32, local_tokens)
    sequence_of = token_index // LEN
    matches = sequence_of[:, None] == lax.iota(jnp.int32, SEQS)[None, :]
    limits = jnp.sum(jnp.where(matches, lengths[None, :], 0), axis=1)
    live_mask = token_index % LEN < limits
    masked = grads_out * live_mask[None, :].astype(jnp.bfloat16)
    out_cols = basis_out.shape[1]
    partial_out = lax.dot_general(
        lax.all_gather(masked, "tp", axis=1, tiled=True),
        basis_out,
        (((0,), (0,)), ((), ())),
        preferred_element_type=jnp.float32,
    )
    rotated_out = lax.psum(partial_out, "wide").astype(jnp.bfloat16)
    partial_in = jnp.dot(
        lax.all_gather(activations, "wide", axis=0, tiled=True),
        basis_in,
        preferred_element_type=jnp.float32,
    )
    rotated_in = lax.psum(partial_in, "tp").astype(jnp.bfloat16)
    outer_side = rotated_out.reshape(SEQS, LEN, out_cols)
    inner_side = rotated_in.reshape(SEQS, LEN, rotated_in.shape[1])
    products = jnp.einsum(
        "nlo,nli->noi", outer_side, inner_side, preferred_element_type=jnp.float32
    )
    summed = jnp.sum(products * products, axis=0)
    return summed / jnp.sum(lengths).astype(jnp.float32)


def solution(mesh):
    placed = (
        P(("layer", "wide"), "tp"),
        P(("layer", "wide"), "tp"),
        P(("layer", "tp"), "wide"),
        P(("layer", "wide"), "tp"),
        P(),
    )
    return jax.shard_map(
        on_device, mesh=mesh, in_specs=placed, out_specs=P(("layer", "tp"), "wide"), check_vma=False
    )
```

profile of v0, /device:TPU:6, one launch (start us, length us, event | category | flops | bytes accessed | tf_op | source)
XLA Modules:
  0.0 358.3 jit_solution(12868663124483192034)
XLA Ops:
  6.5 0.0 copy-start
  6.5 0.0 all-gather.3.cloned.1.call-start
  6.6 0.8 select_reduce_fusion
  7.4 1.6 broadcast_multiply_fusion
  9.0 0.0 all-gather.3.cloned.1.call-update
  9.0 0.0 all-gather.5.cloned.1.call-start
  9.0 0.7 all-gather.5.cloned.1.call-update
  9.7 1.4 reduce_sum.29
  11.8 26.2 %all-gather.3.cloned.1.call-done = bf16[512,1024]{1,0:T(8,128)(2,1)} async-done(((bf16[512,128]{1,0:T(8,128)(2,1)}), bf16[512,1024]{1,0:T(8,128)(2,1)}) %all-gather.3.cloned.1.call-update) | async-done | bytes 1048592 | tf_op jit(solution)/shard_map/all_gather | solution.py:20
  38.1 0.0 copy-done
  38.1 4.6 %fusion = f32[1024,1024]{1,0:T(8,128)} fusion(bf16[512,1024]{1,0:T(8,128)(2,1)} %all-gather.3.cloned.1.call-done, bf16[512,1024]{1,0:T(8,128)(2,1)S(1)} %copy-done), kind=kOutput, calls=%fused_computation.12 | convolution fusion | flops 1073741824 | bytes 6291456 | tf_op jit(solution)/shard_map/dot_general | solution.py:19
  42.7 223.0 %all-reduce.3 = bf16[1024,1024]{1,0:T(8,128)(2,1)S(1)} all-reduce(f32[1024,1024]{1,0:T(8,128)} %fusion), channel_id=1, replica_groups=mesh['layer'=2,'wide'=16,'tp'=8] {'wide'}, use_global_device_ids=true, to_apply=%region_1.2 | all-reduce | flops 1048576 | bytes 6291456 | tf_op jit(solution)/shard_map/psum | solution.py:25
  265.7 5.2 %all-gather.5.cloned.1.call-done = bf16[1024,3584]{1,0:T(8,128)(2,1)} async-done(((bf16[64,3584]{1,0:T(8,128)(2,1)}), bf16[1024,3584]{1,0:T(8,128)(2,1)}) %all-gather.5.cloned.1.call-update) | async-done | bytes 7340048 | tf_op jit(solution)/shard_map/all_gather | solution.py:27
  270.9 13.1 %fusion.1 = f32[1024,896]{1,0:T(8,128)} fusion(bf16[1024,3584]{1,0:T(8,128)(2,1)} %all-gather.5.cloned.1.call-done, bf16[3584,896]{1,0:T(8,128)(2,1)} %param.7), kind=kOutput, calls=%fused_computation.13 | convolution fusion | flops 6576668672 | bytes 17432576 | tf_op jit(solution)/shard_map/dot_general | solution.py:26
  283.9 59.3 %all-reduce.2 = bf16[1024,896]{1,0:T(8,128)(2,1)} all-reduce(f32[1024,896]{1,0:T(8,128)} %fusion.1), channel_id=1, replica_groups=mesh['layer'=2,'wide'=16,'tp'=8] {'tp'}, use_global_device_ids=true, to_apply=%region_2.3 | all-reduce | flops 917504 | bytes 5505024 | tf_op jit(solution)/shard_map/psum | solution.py:31
  343.2 6.2 %multiply_reduce_fusion = f32[1024,896]{1,0:T(8,128)S(1)} fusion(bf16[8,128,1024]{2,1,0:T(8,128)(2,1)S(1)} %bitcast.8, bf16[8,128,896]{2,1,0:T(8,128)(2,1)} %bitcast.9), kind=kOutput, calls=%fused_computation | convolution fusion | flops 1892810752 | bytes 7602176 | tf_op jit(solution)/shard_map/nlo,nli->noi/dot_general | solution.py:34
  349.4 2.1 broadcast_divide_fusion
  (2 shorter events, 0.0 us)
Async XLA Ops:
  6.5 31.5 %copy-start = (bf16[512,1024]{1,0:T(8,128)(2,1)S(1)}, bf16[512,1024]{1,0:T(8,128)(2,1)}, u32[]{:S(2)}) copy-start(bf16[512,1024]{1,0:T(8,128)(2,1)} %param.8) | copy-start | bytes 3145732
  6.5 31.5 %all-gather.3.cloned.1.call-start = ((), (), s32[]{:S(2)}) async-start(), calls=%async_computation | async-start | bytes 1179648 | tf_op jit(solution)/shard_map/all_gather | solution.py:20
  9.0 261.9 %all-gather.5.cloned.1.call-start = ((), (), s32[]{:S(2)}) async-start(), calls=%async_computation.1 | async-start | bytes 7798784 | tf_op jit(solution)/shard_map/all_gather | solution.py:27
Sparse Core Ops, SparseCore 0:
  9.2 28.8 all-gather.2
  40.6 230.1 all-gather.4
where the time goes:
time: 359 us; the launch traced here: 358 us
  blocking collectives  282 us (79%)
  waiting for transfers between devices  32.1 us (9%)
  matrix products  23.8 us (7%)
  between operations  14.1 us (4%)
  other arithmetic  5.88 us (2%)
    psum x1, blocking collectives, on_device(): rotated_out = lax.psum(partial_out, 'wide').astype(jnp.bfloat16)  223 us
    psum x1, blocking collectives, on_device(): rotated_in = lax.psum(partial_in, 'tp').astype(jnp.bfloat16)  59.3 us
    all_gather x1, waiting for transfers between devices, on_device(): lax.all_gather(masked, 'tp', axis=1, tiled=True)  26.2 us
    dot_general x1, matrix products, on_device(): jnp.dot(lax.all_gather(activations, 'wide', axis=0, tiled=True), basis_in...  13.1 us
  transfers between devices with their start and end apart: 2, of which 2 were waited for; matrix products, arithmetic and copies ran while one was open for 2% of the time, Pallas kernels for 0%

commit v1 on v0

v1 whole, which is shorter than its diff:
```python
import jax
import jax.numpy as jnp
from jax import lax
from jax.experimental import pallas as pl
from jax.experimental.pallas import tpu as pltpu
from jax.sharding import PartitionSpec as P

LEN = 128
SEQS = 8
HALF = LEN // 2
Z = 8
RS_DTYPE = jnp.bfloat16


def shift_z(x, step):
    pairs = [(z * 2 + h, (z + step) % Z * 2 + h) for z in range(Z) for h in range(2)]
    return lax.ppermute(x, "wide", pairs)


def swap_x(x):
    return lax.ppermute(x, "wide", [(i, i ^ 1) for i in range(2 * Z)])


def spread(x):
    copies = jnp.broadcast_to(x[None], (8,) + x.shape)
    return lax.all_to_all(copies, "tp", 0, 0, tiled=True)


def after(values, *others):
    return lax.optimization_barrier((values, others))[0]


def partial_out_kernel(order, g_ref, b_ref, o_ref):
    o_ref[0] = lax.dot_general(
        g_ref[0], b_ref[...], (((0,), (0,)), ((), ())), preferred_element_type=jnp.float32
    ).astype(o_ref.dtype)


def partial_out(order, grads, basis):
    _, rows, _ = grads.shape
    cols = basis.shape[1]
    return pl.pallas_call(
        partial_out_kernel,
        out_shape=jax.ShapeDtypeStruct((SEQS, LEN, cols), jnp.float32),
        grid_spec=pltpu.PrefetchScalarGridSpec(
            num_scalar_prefetch=1,
            grid=(SEQS,),
            in_specs=[
                pl.BlockSpec((1, rows, LEN), lambda k, order: (order[k], 0, 0)),
                pl.BlockSpec((rows, cols), lambda k, order: (0, 0)),
            ],
            out_specs=pl.BlockSpec((1, LEN, cols), lambda k, order: (k, 0, 0)),
        ),
        cost_estimate=pl.CostEstimate(
            flops=2 * SEQS * LEN * rows * cols, bytes_accessed=8 * 2**20, transcendentals=0
        ),
    )(order, grads, basis)


def rotate_in(blocks, basis):
    rows = jnp.concatenate(blocks, axis=0)
    return jnp.dot(rows, basis, preferred_element_type=jnp.float32)


def scatter_sum(partial):
    tokens, cols = partial.shape
    pieces = lax.all_to_all(partial.reshape(8, tokens // 8, cols), "tp", 0, 0, tiled=True)
    return jnp.sum(pieces, axis=0).astype(jnp.bfloat16)


def products_kernel(count, *refs):
    scale_ref, base_ref = refs[0], refs[1]
    outs, ins = refs[2 : 2 + 2 * count], refs[2 + 2 * count : 2 + 4 * count]
    o_ref = refs[-1]
    total = base_ref[...] if base_ref is not None else None
    for n in range(count):
        left = jnp.concatenate([outs[2 * n][...], outs[2 * n + 1][...]], axis=0)
        right = jnp.concatenate([ins[2 * n][...], ins[2 * n + 1][...]], axis=0)
        product = lax.dot_general(
            left, right, (((0,), (0,)), ((), ())), preferred_element_type=jnp.float32
        )
        total = product * product if total is None else total + product * product
    if scale_ref is not None:
        total = total / scale_ref[0]
    o_ref[...] = total


def products(base, pairs, scale=None):
    out_cols = pairs[0][0][0].shape[1]
    in_cols = pairs[0][1][0].shape[1]
    tile = 128
    count = len(pairs)
    outs = [block for pair in pairs for block in pair[0]]
    ins = [block for pair in pairs for block in pair[1]]
    args, specs = [], []
    if scale is not None:
        args.append(scale.reshape(1))
        specs.append(pl.BlockSpec(memory_space=pltpu.SMEM))
    if base is not None:
        args.append(base)
        specs.append(pl.BlockSpec((tile, in_cols), lambda i: (i, 0)))
    args += outs + ins
    specs += [pl.BlockSpec((HALF, tile), lambda i: (0, i))] * len(outs)
    specs += [pl.BlockSpec((HALF, in_cols), lambda i: (0, 0))] * len(ins)

    def kernel(*refs):
        refs = list(refs)
        scale_ref = refs.pop(0) if scale is not None else None
        base_ref = refs.pop(0) if base is not None else None
        products_kernel(count, scale_ref, base_ref, *refs)

    return pl.pallas_call(
        kernel,
        out_shape=jax.ShapeDtypeStruct((out_cols, in_cols), jnp.float32),
        grid=(out_cols // tile,),
        in_specs=specs,
        out_specs=pl.BlockSpec((tile, in_cols), lambda i: (i, 0)),
        compiler_params=pltpu.CompilerParams(vmem_limit_bytes=32 * 2**20),
        cost_estimate=pl.CostEstimate(
            flops=4 * count * LEN * out_cols * in_cols, bytes_accessed=8 * 2**20, transcendentals=0
        ),
    )(*args)


def on_device(activations, grads_out, basis_in, basis_out, lengths):
    place = lax.axis_index("wide")
    z, h = place // 2, place % 2
    order = (z + lax.iota(jnp.int32, SEQS)) % SEQS

    a, c = {}, {}
    a[0] = activations
    a[-1], a[1], c[0] = shift_z(a[0], 1), shift_z(a[0], -1), swap_x(a[0])
    grads = spread(grads_out)
    a[-1], a[1], c[0], grads = lax.optimization_barrier((a[-1], a[1], c[0], grads))

    a[-2], a[2], c[1] = shift_z(a[-1], 1), shift_z(a[1], -1), swap_x(a[1])
    part = partial_out(order, grads, basis_out)
    send_p, send_m = part[4].astype(RS_DTYPE), part[5].astype(RS_DTYPE)
    rs_p, rs_m = shift_z(send_p, 1), shift_z(send_m, -1)
    in1 = rotate_in([a[0], c[0], a[1], a[-1]], after(basis_in, send_p, send_m))
    a[-2], a[2], c[1], rs_p, rs_m, in1 = lax.optimization_barrier((a[-2], a[2], c[1], rs_p, rs_m, in1))

    a[-3], a[3], c[2] = shift_z(a[-2], 1), shift_z(a[2], -1), swap_x(a[2])
    send_p = (rs_p.astype(jnp.float32) + part[3]).astype(RS_DTYPE)
    send_m = (rs_m.astype(jnp.float32) + part[6]).astype(RS_DTYPE)
    rs_p, rs_m = shift_z(send_p, 1), shift_z(send_m, -1)
    sum1 = scatter_sum(in1)
    in2 = rotate_in([a[-2], a[2], c[1]], after(basis_in, send_p, send_m))
    a[-3], a[3], c[2], rs_p, rs_m, sum1, in2 = lax.optimization_barrier(
        (a[-3], a[3], c[2], rs_p, rs_m, sum1, in2)
    )

    a[4], c[3], c[-2] = shift_z(a[-3], 1), shift_z(c[2], -1), swap_x(a[-2])
    send_p = (rs_p.astype(jnp.float32) + part[2]).astype(RS_DTYPE)
    send_m = (rs_m.astype(jnp.float32) + part[7]).astype(RS_DTYPE)
    rs_p, rs_m = shift_z(send_p, 1), shift_z(send_m, -1)
    all1 = spread(sum1)
    in3 = rotate_in([a[-3], a[3], c[2]], after(basis_in, send_p, send_m))
    a[4], c[3], c[-2], rs_p, rs_m, all1, in3 = lax.optimization_barrier(
        (a[4], c[3], c[-2], rs_p, rs_m, all1, in3)
    )

    c[-3], c[4], c[-1] = shift_z(c[-2], 1), shift_z(c[3], -1), swap_x(a[-1])
    send_p = (rs_p.astype(jnp.float32) + part[1]).astype(RS_DTYPE)
    own = part[0] + rs_m.astype(jnp.float32)
    rs_p = shift_z(send_p, 1)
    sum23 = scatter_sum(jnp.concatenate([in2, in3], axis=0))
    in4 = rotate_in([a[4], c[3], c[-2]], after(basis_in, send_p, own))
    c[-3], c[4], c[-1], rs_p, sum23, in4 = lax.optimization_barrier((c[-3], c[4], c[-1], rs_p, sum23, in4))

    own = own + rs_p.astype(jnp.float32)
    cols = own.shape[1]
    mine = lax.dynamic_slice(own, (h * HALF, 0), (HALF, cols))
    theirs = lax.dynamic_slice(own, ((1 - h) * HALF, 0), (HALF, cols))
    got = swap_x(theirs)
    in5 = rotate_in([c[-3], c[4], c[-1]], after(basis_in, theirs))
    token = lax.iota(jnp.int32, HALF) + h * HALF
    live = token < lax.dynamic_index_in_dim(lengths, z, 0, keepdims=False)
    b, d = {}, {}
    b[0] = jnp.where(live[:, None], mine + got, 0.0).astype(jnp.bfloat16)
    b[0], in5 = lax.optimization_barrier((b[0], in5))

    b[-1], b[1], d[0] = shift_z(b[0], 1), shift_z(b[0], -1), swap_x(b[0])
    sum45 = scatter_sum(jnp.concatenate([in4, in5], axis=0))
    all23 = spread(sum23)
    b[-1], b[1], d[0] = lax.optimization_barrier((b[-1], b[1], d[0]))
    b[-2], b[2], d[1] = shift_z(b[-1], 1), shift_z(b[1], -1), swap_x(b[1])
    b[-2], b[2], d[1], sum45, all23 = lax.optimization_barrier((b[-2], b[2], d[1], sum45, all23))
    all45 = spread(sum45)
    b[-3], b[3], d[2] = shift_z(b[-2], 1), shift_z(b[2], -1), swap_x(b[2])
    b[-3], b[3], d[2] = lax.optimization_barrier((b[-3], b[3], d[2]))
    b[4], d[3], d[-2] = shift_z(b[-3], 1), shift_z(d[2], -1), swap_x(b[-2])
    b[4], d[3], d[-2] = lax.optimization_barrier((b[4], d[3], d[-2]))
    d[-3], d[4], d[-1] = shift_z(d[-2], 1), shift_z(d[3], -1), swap_x(b[-1])

    ins = {}
    wide = basis_in.shape[1]
    first = all1.reshape(4, HALF, wide)
    second = all23.reshape(6, HALF, wide)
    third = all45.reshape(6, HALF, wide)
    ia = {0: first[0], 1: first[2], -1: first[3], -2: second[0], 2: second[1], -3: second[3], 3: second[4], 4: third[0]}
    ic = {0: first[1], 1: second[2], 2: second[5], 3: third[1], -2: third[2], -3: third[3], 4: third[4], -1: third[5]}
    pair = lambda k: ((b[k], d[k]), (ia[k], ic[k]))
    total = jnp.sum(lengths).astype(jnp.float32)
    early = products(None, [pair(0), pair(1), pair(2)])
    return products(early, [pair(3), pair(-2), pair(-3), pair(4), pair(-1)], total)


def solution(mesh):
    placed = (
        P(("layer", "wide"), "tp"),
        P(("layer", "wide"), "tp"),
        P(("layer", "tp"), "wide"),
        P(("layer", "wide"), "tp"),
        P(),
    )
    return jax.shard_map(
        on_device, mesh=mesh, in_specs=placed, out_specs=P(("layer", "tp"), "wide"), check_vma=False
    )
```

time: 359 us -> 250 us (0.70)
  the two profiles are of different devices: /device:TPU:6 before, /device:TPU:8 now
where the time goes in v1:
time: 250 us; the launch traced here: 246 us
  starting transfers between devices  105 us (42%)
  waiting for transfers between devices  52.2 us (21%)
  matrix products  25.3 us (10%)
  blocking collectives  22.8 us (9%)
  Pallas kernels  17.5 us (7%)
  other arithmetic  10.7 us (4%)
  local copies, waits for them, and re-layouts  10.6 us (4%)
    ppermute x27, starting transfers between devices, shift_z(): return lax.ppermute(x, 'wide', pairs)  40.9 us
    ppermute x11, starting transfers between devices, swap_x(): return lax.ppermute(x, 'wide', [(i, i ^ 1) for i in range(2 * Z)])  34 us
    ppermute x27, waiting for transfers between devices, shift_z(): return lax.ppermute(x, 'wide', pairs)  30.8 us
    dot_general x5, matrix products, rotate_in(): return jnp.dot(rows, basis, preferred_element_type=jnp.float32)  25.3 us
    all_to_all x1, blocking collectives, scatter_sum(): lax.all_to_all(partial.reshape(8, tokens // 8, cols), 'tp', 0, 0, tiled=T...  22.8 us
    all_to_all x4, starting transfers between devices, spread(): return lax.all_to_all(copies, 'tp', 0, 0, tiled=True)  20.8 us
    ppermute x11, waiting for transfers between devices, swap_x(): return lax.ppermute(x, 'wide', [(i, i ^ 1) for i in range(2 * Z)])  14.3 us
    all_to_all x2, starting transfers between devices, scatter_sum(): lax.all_to_all(partial.reshape(8, tokens // 8, cols), 'tp', 0, 0, tiled=T...  9.61 us
  transfers between devices with their start and end apart: 44, of which 17 were waited for; matrix products, arithmetic and copies ran while one was open for 15% of the time, Pallas kernels for 5%

profile of v1, /device:TPU:8, one launch (start us, length us, event | category | flops | bytes accessed | tf_op | source)
XLA Modules:
  0.0 245.6 jit_solution(16700753312566951106)
XLA Ops:
  2.1 5.7 %all-to-all-start = ((bf16[8,512,128]{2,1,0:T(8,128)(2,1)}), bf16[8,512,128]{2,1,0:T(8,128)(2,1)S(1)}, u32[]{:S(2)}, u32[]{:S(2)}) async-start(bf16[8,512,128]{2,1,0:T(8,128)(2,1)} %broadcast_in_dim.21), calls=%async_computation | async-start | bytes 2097152 | tf_op jit(solution)/shard_map/all_to_all | solution.py:26
  8.9 4.0 %collective-permute-start.1 = (bf16[64,3584]{1,0:T(8,128)(2,1)S(1)}, bf16[64,3584]{1,0:T(8,128)(2,1)S(1)}, u32[]{:S(2)}, u32[]{:S(2)}) collective-permute-start(bf16[64,3584]{1,0:T(8,128)(2,1)S(1)} %copy-done.6), channel_id=1, source_target_pairs={{0,112},{8,120},{16,0},{24,8},{32,16},{40,24},{48,32},{56,40},{64,... | collective-permute-start | bytes 1376264 | tf_op jit(solution)/shard_map/ppermute | solution.py:17
  12.9 3.0 %collective-permute-start.2 = (bf16[64,3584]{1,0:T(8,128)(2,1)S(1)}, bf16[64,3584]{1,0:T(8,128)(2,1)S(1)}, u32[]{:S(2)}, u32[]{:S(2)}) collective-permute-start(bf16[64,3584]{1,0:T(8,128)(2,1)S(1)} %copy-done.6), channel_id=1, source_target_pairs={{0,8},{8,0},{16,24},{24,16},{32,40},{40,32},{48,56},{56,48},{64,72... | collective-permute-start | bytes 1376264 | tf_op jit(solution)/shard_map/ppermute | solution.py:21
  16.5 7.3 %collective-permute-done = bf16[64,3584]{1,0:T(8,128)(2,1)} collective-permute-done((bf16[64,3584]{1,0:T(8,128)(2,1)S(1)}, bf16[64,3584]{1,0:T(8,128)(2,1)}, u32[]{:S(2)}, u32[]{:S(2)}) %collective-permute-start) | collective-permute-done | bytes 458784 | tf_op jit(solution)/shard_map/ppermute | solution.py:17
  23.8 2.9 %collective-permute-done.2 = bf16[64,3584]{1,0:T(8,128)(2,1)S(1)} collective-permute-done((bf16[64,3584]{1,0:T(8,128)(2,1)S(1)}, bf16[64,3584]{1,0:T(8,128)(2,1)S(1)}, u32[]{:S(2)}, u32[]{:S(2)}) %collective-permute-start.2) | collective-permute-done | bytes 458784 | tf_op jit(solution)/shard_map/ppermute | solution.py:21
  28.4 3.0 %collective-permute-start.5 = (bf16[64,3584]{1,0:T(8,128)(2,1)S(1)}, bf16[64,3584]{1,0:T(8,128)(2,1)S(1)}, u32[]{:S(2)}, u32[]{:S(2)}) collective-permute-start(bf16[64,3584]{1,0:T(8,128)(2,1)S(1)} %collective-permute-done.1), channel_id=1, source_target_pairs={{0,8},{8,0},{16,24},{24,16},{32,40},{40,32},{48,56},{56,48},{64,72... | collective-permute-start | bytes 1376264 | tf_op jit(solution)/shard_map/ppermute | solution.py:21
  31.4 8.1 %shard_map.55 = f32[8,128,1024]{2,1,0:T(8,128)} custom-call(s32[8]{0:T(128)} %and_select_fusion.order, bf16[8,512,128]{2,1,0:T(8,128)(2,1)} %copy-done.2, bf16[512,1024]{1,0:T(8,128)(2,1)} %b_ref.1), custom_call_target="tpu_custom_call" | custom-call | flops 1073741824 | bytes 8388608 | tf_op jit(solution)/shard_map/pallas_call | solution.py:42
  45.4 6.0 %fusion = f32[256,896]{1,0:T(8,128)} fusion(bf16[3584,896]{1,0:T(8,128)(2,1)} %param.7, bf16[64,3584]{1,0:T(8,128)(2,1)} %collective-permute-done, bf16[64,3584]{1,0:T(8,128)(2,1)S(1)} %collective-permute-done.1, bf16[64,3584]{1,0:T(8,128)(2,1)S(1)} %collective-permute-done.2, bf16[64,3584]{1,0:T(8,128)(2,1)S(1)} %copy-done.6), kind=kOutput, calls=%fused_computation | convolution fusion | flops 1651507200 | bytes 9175040 | tf_op jit(solution)/shard_map/dot_general | solution.py:62
  52.5 7.2 %collective-permute-done.3 = bf16[64,3584]{1,0:T(8,128)(2,1)} collective-permute-done((bf16[64,3584]{1,0:T(8,128)(2,1)}, bf16[64,3584]{1,0:T(8,128)(2,1)}, u32[]{:S(2)}, u32[]{:S(2)}) %collective-permute-start.3) | collective-permute-done | bytes 458784 | tf_op jit(solution)/shard_map/ppermute | solution.py:17
  59.7 4.8 %all-to-all-start.1 = ((f32[8,32,896]{2,1,0:T(8,128)}), f32[8,32,896]{2,1,0:T(8,128)S(1)}, u32[]{:S(2)}, u32[]{:S(2)}) async-start(f32[8,32,896]{2,1,0:T(8,128)} %bitcast.7), calls=%async_computation.1 | async-start | bytes 1835008 | tf_op jit(solution)/shard_map/all_to_all | solution.py:67
  65.9 3.2 %collective-permute-start.12 = (bf16[128,1024]{1,0:T(8,128)(2,1)S(1)}, bf16[128,1024]{1,0:T(8,128)(2,1)S(1)}, u32[]{:S(2)}, u32[]{:S(2)}) collective-permute-start(bf16[128,1024]{1,0:T(8,128)(2,1)S(1)} %get-tuple-element.111), channel_id=1, source_target_pairs={{0,112},{8,120},{16,0},{24,8},{32,16},{40,24},{48,32},{56,40},{64,... | collective-permute-start | bytes 786440 | tf_op jit(solution)/shard_map/ppermute | solution.py:17
  71.9 4.7 %fusion.8 = f32[192,896]{1,0:T(8,128)S(1)} fusion(bf16[3584,896]{1,0:T(8,128)(2,1)} %param.7, bf16[64,3584]{1,0:T(8,128)(2,1)S(1)} %collective-permute-done.5, bf16[64,3584]{1,0:T(8,128)(2,1)} %collective-permute-done.4, bf16[64,3584]{1,0:T(8,128)(2,1)} %collective-permute-done.3), kind=kOutput, calls=%fused_computation.8 | convolution fusion | flops 1237254144 | bytes 8486912 | tf_op jit(solution)/shard_map/dot_general | solution.py:62
  79.8 4.1 %collective-permute-done.10 = bf16[64,3584]{1,0:T(8,128)(2,1)} collective-permute-done((bf16[64,3584]{1,0:T(8,128)(2,1)}, bf16[64,3584]{1,0:T(8,128)(2,1)}, u32[]{:S(2)}, u32[]{:S(2)}) %collective-permute-start.10) | collective-permute-done | bytes 458784 | tf_op jit(solution)/shard_map/ppermute | solution.py:21
  86.8 3.2 %collective-permute-start.17 = (bf16[128,1024]{1,0:T(8,128)(2,1)S(1)}, bf16[128,1024]{1,0:T(8,128)(2,1)S(1)}, u32[]{:S(2)}, u32[]{:S(2)}) collective-permute-start(bf16[128,1024]{1,0:T(8,128)(2,1)S(1)} %get-tuple-element.109), channel_id=1, source_target_pairs={{0,112},{8,120},{16,0},{24,8},{32,16},{40,24},{48,32},{56,40},{64,... | collective-permute-start | bytes 786440 | tf_op jit(solution)/shard_map/ppermute | solution.py:17
  90.9 4.8 %all-to-all-start.2 = ((bf16[8,32,896]{2,1,0:T(8,128)(2,1)}), bf16[8,32,896]{2,1,0:T(8,128)(2,1)S(1)}, u32[]{:S(2)}, u32[]{:S(2)}) async-start(bf16[8,32,896]{2,1,0:T(8,128)(2,1)} %broadcast_in_dim.22), calls=%async_computation.2 | async-start | bytes 917504 | tf_op jit(solution)/shard_map/all_to_all | solution.py:26
  95.7 3.2 %collective-permute-start.14 = (bf16[64,3584]{1,0:T(8,128)(2,1)}, bf16[64,3584]{1,0:T(8,128)(2,1)}, u32[]{:S(2)}, u32[]{:S(2)}) collective-permute-start(bf16[64,3584]{1,0:T(8,128)(2,1)} %collective-permute-done.10), channel_id=1, source_target_pairs={{0,112},{8,120},{16,0},{24,8},{32,16},{40,24},{48,32},{56,40},{64,... | collective-permute-start | bytes 1376264 | tf_op jit(solution)/shard_map/ppermute | solution.py:17
  98.9 4.9 %fusion.14 = f32[192,896]{1,0:T(8,128)S(1)} fusion(bf16[3584,896]{1,0:T(8,128)(2,1)} %param.7, bf16[64,3584]{1,0:T(8,128)(2,1)} %collective-permute-done.10, bf16[64,3584]{1,0:T(8,128)(2,1)} %collective-permute-done.9, bf16[64,3584]{1,0:T(8,128)(2,1)} %collective-permute-done.8), kind=kOutput, calls=%fused_computation.14 | convolution fusion | flops 1237254144 | bytes 8486912 | tf_op jit(solution)/shard_map/dot_general | solution.py:62
  103.9 5.9 %collective-permute-done.13 = bf16[64,3584]{1,0:T(8,128)(2,1)} collective-permute-done((bf16[64,3584]{1,0:T(8,128)(2,1)}, bf16[64,3584]{1,0:T(8,128)(2,1)}, u32[]{:S(2)}, u32[]{:S(2)}) %collective-permute-start.13) | collective-permute-done | bytes 458784 | tf_op jit(solution)/shard_map/ppermute | solution.py:17
  110.9 4.8 %all-to-all-start.3 = ((f32[8,48,896]{2,1,0:T(8,128)}), f32[8,48,896]{2,1,0:T(8,128)S(1)}, u32[]{:S(2)}, u32[]{:S(2)}) async-start(f32[8,48,896]{2,1,0:T(8,128)} %bitcast.11), calls=%async_computation.3 | async-start | bytes 2752512 | tf_op jit(solution)/shard_map/all_to_all | solution.py:67
  122.8 4.9 %fusion.20 = f32[192,896]{1,0:T(8,128)S(1)} fusion(bf16[3584,896]{1,0:T(8,128)(2,1)} %param.7, bf16[64,3584]{1,0:T(8,128)(2,1)} %copy-done.7, bf16[64,3584]{1,0:T(8,128)(2,1)} %collective-permute-done.14, bf16[64,3584]{1,0:T(8,128)(2,1)} %collective-permute-done.13), kind=kOutput, calls=%fused_computation.21 | convolution fusion | flops 1237254144 | bytes 8486912 | tf_op jit(solution)/shard_map/dot_general | solution.py:62
  127.7 6.1 %all-to-all-done.3 = f32[8,48,896]{2,1,0:T(8,128)S(1)} async-done(((f32[8,48,896]{2,1,0:T(8,128)}), f32[8,48,896]{2,1,0:T(8,128)S(1)}, u32[]{:S(2)}, u32[]{:S(2)}) %all-to-all-start.3) | async-done | bytes 1376288 | tf_op jit(solution)/shard_map/all_to_all | solution.py:67
  134.5 4.1 %collective-permute-done.18 = bf16[64,3584]{1,0:T(8,128)(2,1)} collective-permute-done((bf16[64,3584]{1,0:T(8,128)(2,1)}, bf16[64,3584]{1,0:T(8,128)(2,1)}, u32[]{:S(2)}, u32[]{:S(2)}) %collective-permute-start.18) | collective-permute-done | bytes 458784 | tf_op jit(solution)/shard_map/ppermute | solution.py:17
  138.7 12.5 %collective-permute-start.22 = (f32[64,1024]{1,0:T(8,128)S(1)}, f32[64,1024]{1,0:T(8,128)S(1)}, u32[]{:S(2)}, u32[]{:S(2)}) collective-permute-start(f32[64,1024]{1,0:T(8,128)S(1)} %constant_dynamic-slice_fusion), channel_id=1, source_target_pairs={{0,8},{8,0},{16,24},{24,16},{32,40},{40,32},{48,56},{56,48},{64,72... | collective-permute-start | bytes 786440 | tf_op jit(solution)/shard_map/ppermute | solution.py:21
  151.2 4.9 %fusion.26 = f32[192,896]{1,0:T(8,128)S(1)} fusion(bf16[3584,896]{1,0:T(8,128)(2,1)} %param.7, bf16[64,3584]{1,0:T(8,128)(2,1)} %collective-permute-done.20, bf16[64,3584]{1,0:T(8,128)(2,1)} %collective-permute-done.19, bf16[64,3584]{1,0:T(8,128)(2,1)} %collective-permute-done.18), kind=kOutput, calls=%fused_computation.27 | convolution fusion | flops 1237254144 | bytes 8486912 | tf_op jit(solution)/shard_map/dot_general | solution.py:62
  157.3 22.8 %all_to_all.35 = f32[8,48,896]{2,1,0:T(8,128)S(1)} all-to-all(f32[8,48,896]{2,1,0:T(8,128)S(1)} %bitcast.82), channel_id=1, replica_groups=mesh['layer'=2,'wide'=16,'tp'=8] {'tp'}, dimensions={0} | all-to-all | bytes 2752512 | tf_op jit(solution)/shard_map/all_to_all | solution.py:67
  181.0 5.6 %all-to-all-start.5 = ((bf16[8,48,896]{2,1,0:T(8,128)(2,1)}), bf16[8,48,896]{2,1,0:T(8,128)(2,1)}, u32[]{:S(2)}, u32[]{:S(2)}) async-start(bf16[8,48,896]{2,1,0:T(8,128)(2,1)} %broadcast_in_dim.24), calls=%async_computation.5 | async-start | bytes 1376256 | tf_op jit(solution)/shard_map/all_to_all | solution.py:26
  186.6 3.2 %collective-permute-start.24 = (bf16[64,1024]{1,0:T(8,128)(2,1)S(1)}, bf16[64,1024]{1,0:T(8,128)(2,1)S(1)}, u32[]{:S(2)}, u32[]{:S(2)}) collective-permute-start(bf16[64,1024]{1,0:T(8,128)(2,1)S(1)} %select_convert_fusion.refs_0_), channel_id=1, source_target_pairs={{0,112},{8,120},{16,0},{24,8},{32,16},{40,24},{48,32},{56,40},{64,... | collective-permute-start | bytes 393224 | tf_op jit(solution)/shard_map/ppermute | solution.py:17
  193.4 3.0 %collective-permute-done.25.refs_1_ = bf16[64,1024]{1,0:T(8,128)(2,1)S(1)} collective-permute-done((bf16[64,1024]{1,0:T(8,128)(2,1)S(1)}, bf16[64,1024]{1,0:T(8,128)(2,1)S(1)}, u32[]{:S(2)}, u32[]{:S(2)}) %collective-permute-start.25) | collective-permute-done | bytes 131104 | tf_op jit(solution)/shard_map/ppermute | solution.py:21
  196.3 3.2 %collective-permute-start.27 = (bf16[64,1024]{1,0:T(8,128)(2,1)S(1)}, bf16[64,1024]{1,0:T(8,128)(2,1)S(1)}, u32[]{:S(2)}, u32[]{:S(2)}) collective-permute-start(bf16[64,1024]{1,0:T(8,128)(2,1)S(1)} %collective-permute-done.24.refs_2_), channel_id=1, source_target_pairs={{0,112},{8,120},{16,0},{24,8},{32,16},{40,24},{48,32},{56,40},{64,... | collective-permute-start | bytes 393224 | tf_op jit(solution)/shard_map/ppermute | solution.py:17
  207.0 4.8 %all-to-all-start.6 = ((bf16[8,48,896]{2,1,0:T(8,128)(2,1)}), bf16[8,48,896]{2,1,0:T(8,128)(2,1)S(1)}, u32[]{:S(2)}, u32[]{:S(2)}) async-start(bf16[8,48,896]{2,1,0:T(8,128)(2,1)} %broadcast_in_dim.42), calls=%async_computation.6 | async-start | bytes 1376256 | tf_op jit(solution)/shard_map/all_to_all | solution.py:26
  225.8 3.4 %shard_map.56.refs_1_ = f32[1024,896]{1,0:T(8,128)S(1)} custom-call(bf16[64,1024]{1,0:T(8,128)(2,1)S(1)} %select_convert_fusion.refs_0_, bf16[64,1024]{1,0:T(8,128)(2,1)S(1)} %collective-permute-done.25.refs_1_, bf16[64,1024]{1,0:T(8,128)(2,1)S(1)} %collective-permute-done.24.refs_2_, bf16[64,1024]{1,0:T(8,128)(2,1)S(1)} %collective-permute-done.28.refs_3_, ...), custom_call_target="tpu_custom_call" | custom-call | flops 1409286144 | bytes 8388608 | tf_op jit(solution)/shard_map/pallas_call | solution.py:112
  239.4 6.0 %shard_map.57 = f32[1024,896]{1,0:T(8,128)} custom-call(f32[1]{0:T(128)} %bitcast.refs_0_, f32[1024,896]{1,0:T(8,128)S(1)} %copy-done.1, bf16[64,1024]{1,0:T(8,128)(2,1)S(1)} %collective-permute-done.30.refs_2_, bf16[64,1024]{1,0:T(8,128)(2,1)S(1)} %collective-permute-done.33.refs_3_, bf16[64,1024]{1,0:T(8,128)(2,1)S(1)} %collective-permute-done.26.refs_4_, ...), custom_call_target="tpu_custom_call" | custom-call | flops 2348810240 | bytes 8388608 | tf_op jit(solution)/shard_map/pallas_call | solution.py:112
  (107 shorter events, 69.1 us)
Async XLA Ops:
  2.1 24.7 %all-to-all-start = ((bf16[8,512,128]{2,1,0:T(8,128)(2,1)}), bf16[8,512,128]{2,1,0:T(8,128)(2,1)S(1)}, u32[]{:S(2)}, u32[]{:S(2)}) async-start(bf16[8,512,128]{2,1,0:T(8,128)(2,1)} %broadcast_in_dim.21), calls=%async_computation | async-start | bytes 2097152 | tf_op jit(solution)/shard_map/all_to_all | solution.py:26
  7.7 16.1 %collective-permute-start = (bf16[64,3584]{1,0:T(8,128)(2,1)S(1)}, bf16[64,3584]{1,0:T(8,128)(2,1)}, u32[]{:S(2)}, u32[]{:S(2)}) collective-permute-start(bf16[64,3584]{1,0:T(8,128)(2,1)S(1)} %copy-done.6), channel_id=1, source_target_pairs={{0,16},{8,24},{16,32},{24,40},{32,48},{40,56},{48,64},{56,72},{64,... | collective-permute-start | bytes 1376264 | tf_op jit(solution)/shard_map/ppermute | solution.py:17
  8.9 14.9 %collective-permute-start.1 = (bf16[64,3584]{1,0:T(8,128)(2,1)S(1)}, bf16[64,3584]{1,0:T(8,128)(2,1)S(1)}, u32[]{:S(2)}, u32[]{:S(2)}) collective-permute-start(bf16[64,3584]{1,0:T(8,128)(2,1)S(1)} %copy-done.6), channel_id=1, source_target_pairs={{0,112},{8,120},{16,0},{24,8},{32,16},{40,24},{48,32},{56,40},{64,... | collective-permute-start | bytes 1376264 | tf_op jit(solution)/shard_map/ppermute | solution.py:17
  12.9 13.8 %collective-permute-start.2 = (bf16[64,3584]{1,0:T(8,128)(2,1)S(1)}, bf16[64,3584]{1,0:T(8,128)(2,1)S(1)}, u32[]{:S(2)}, u32[]{:S(2)}) collective-permute-start(bf16[64,3584]{1,0:T(8,128)(2,1)S(1)} %copy-done.6), channel_id=1, source_target_pairs={{0,8},{8,0},{16,24},{24,16},{32,40},{40,32},{48,56},{56,48},{64,72... | collective-permute-start | bytes 1376264 | tf_op jit(solution)/shard_map/ppermute | solution.py:21
  26.7 32.9 %collective-permute-start.4 = (bf16[64,3584]{1,0:T(8,128)(2,1)S(1)}, bf16[64,3584]{1,0:T(8,128)(2,1)}, u32[]{:S(2)}, u32[]{:S(2)}) collective-permute-start(bf16[64,3584]{1,0:T(8,128)(2,1)S(1)} %collective-permute-done.1), channel_id=1, source_target_pairs={{0,112},{8,120},{16,0},{24,8},{32,16},{40,24},{48,32},{56,40},{64,... | collective-permute-start | bytes 1376264 | tf_op jit(solution)/shard_map/ppermute | solution.py:17
  28.4 31.3 %collective-permute-start.5 = (bf16[64,3584]{1,0:T(8,128)(2,1)S(1)}, bf16[64,3584]{1,0:T(8,128)(2,1)S(1)}, u32[]{:S(2)}, u32[]{:S(2)}) collective-permute-start(bf16[64,3584]{1,0:T(8,128)(2,1)S(1)} %collective-permute-done.1), channel_id=1, source_target_pairs={{0,8},{8,0},{16,24},{24,16},{32,40},{40,32},{48,56},{56,48},{64,72... | collective-permute-start | bytes 1376264 | tf_op jit(solution)/shard_map/ppermute | solution.py:21
  42.1 10.4 %collective-permute-start.6 = (bf16[128,1024]{1,0:T(8,128)(2,1)S(1)}, bf16[128,1024]{1,0:T(8,128)(2,1)S(1)}, u32[]{:S(2)}, u32[]{:S(2)}) collective-permute-start(bf16[128,1024]{1,0:T(8,128)(2,1)S(1)} %get-tuple-element.114), channel_id=1, source_target_pairs={{0,16},{8,24},{16,32},{24,40},{32,48},{40,56},{48,64},{56,72},{64,... | collective-permute-start | bytes 786440 | tf_op jit(solution)/shard_map/ppermute | solution.py:17
  42.5 10.0 %collective-permute-start.7 = (bf16[128,1024]{1,0:T(8,128)(2,1)S(1)}, bf16[128,1024]{1,0:T(8,128)(2,1)S(1)}, u32[]{:S(2)}, u32[]{:S(2)}) collective-permute-start(bf16[128,1024]{1,0:T(8,128)(2,1)S(1)} %get-tuple-element.113), channel_id=1, source_target_pairs={{0,112},{8,120},{16,0},{24,8},{32,16},{40,24},{48,32},{56,40},{64,... | collective-permute-start | bytes 786440 | tf_op jit(solution)/shard_map/ppermute | solution.py:17
  45.4 14.3 %collective-permute-start.3 = (bf16[64,3584]{1,0:T(8,128)(2,1)}, bf16[64,3584]{1,0:T(8,128)(2,1)}, u32[]{:S(2)}, u32[]{:S(2)}) collective-permute-start(bf16[64,3584]{1,0:T(8,128)(2,1)} %collective-permute-done), channel_id=1, source_target_pairs={{0,16},{8,24},{16,32},{24,40},{32,48},{40,56},{48,64},{56,72},{64,... | collective-permute-start | bytes 1376264 | tf_op jit(solution)/shard_map/ppermute | solution.py:17
  59.7 17.9 %all-to-all-start.1 = ((f32[8,32,896]{2,1,0:T(8,128)}), f32[8,32,896]{2,1,0:T(8,128)S(1)}, u32[]{:S(2)}, u32[]{:S(2)}) async-start(f32[8,32,896]{2,1,0:T(8,128)} %bitcast.7), calls=%async_computation.1 | async-start | bytes 1835008 | tf_op jit(solution)/shard_map/all_to_all | solution.py:67
  65.8 11.8 %collective-permute-start.11 = (bf16[128,1024]{1,0:T(8,128)(2,1)S(1)}, bf16[128,1024]{1,0:T(8,128)(2,1)S(1)}, u32[]{:S(2)}, u32[]{:S(2)}) collective-permute-start(bf16[128,1024]{1,0:T(8,128)(2,1)S(1)} %get-tuple-element.112), channel_id=1, source_target_pairs={{0,16},{8,24},{16,32},{24,40},{32,48},{40,56},{48,64},{56,72},{64,... | collective-permute-start | bytes 786440 | tf_op jit(solution)/shard_map/ppermute | solution.py:17
  65.9 13.9 %collective-permute-start.12 = (bf16[128,1024]{1,0:T(8,128)(2,1)S(1)}, bf16[128,1024]{1,0:T(8,128)(2,1)S(1)}, u32[]{:S(2)}, u32[]{:S(2)}) collective-permute-start(bf16[128,1024]{1,0:T(8,128)(2,1)S(1)} %get-tuple-element.111), channel_id=1, source_target_pairs={{0,112},{8,120},{16,0},{24,8},{32,16},{40,24},{48,32},{56,40},{64,... | collective-permute-start | bytes 786440 | tf_op jit(solution)/shard_map/ppermute | solution.py:17
  69.1 14.8 %collective-permute-start.10 = (bf16[64,3584]{1,0:T(8,128)(2,1)}, bf16[64,3584]{1,0:T(8,128)(2,1)}, u32[]{:S(2)}, u32[]{:S(2)}) collective-permute-start(bf16[64,3584]{1,0:T(8,128)(2,1)} %collective-permute-done.4), channel_id=1, source_target_pairs={{0,8},{8,0},{16,24},{24,16},{32,40},{40,32},{48,56},{56,48},{64,72... | collective-permute-start | bytes 1376264 | tf_op jit(solution)/shard_map/ppermute | solution.py:21
  69.6 15.8 %collective-permute-start.9 = (bf16[64,3584]{1,0:T(8,128)(2,1)}, bf16[64,3584]{1,0:T(8,128)(2,1)}, u32[]{:S(2)}, u32[]{:S(2)}) collective-permute-start(bf16[64,3584]{1,0:T(8,128)(2,1)} %collective-permute-done.4), channel_id=1, source_target_pairs={{0,112},{8,120},{16,0},{24,8},{32,16},{40,24},{48,32},{56,40},{64,... | collective-permute-start | bytes 1376264 | tf_op jit(solution)/shard_map/ppermute | solution.py:17
  69.6 15.8 %collective-permute-start.8 = (bf16[64,3584]{1,0:T(8,128)(2,1)}, bf16[64,3584]{1,0:T(8,128)(2,1)}, u32[]{:S(2)}, u32[]{:S(2)}) collective-permute-start(bf16[64,3584]{1,0:T(8,128)(2,1)} %collective-permute-done.3), channel_id=1, source_target_pairs={{0,16},{8,24},{16,32},{24,40},{32,48},{40,56},{48,64},{56,72},{64,... | collective-permute-start | bytes 1376264 | tf_op jit(solution)/shard_map/ppermute | solution.py:17
  77.7 26.1 %collective-permute-start.15 = (bf16[64,3584]{1,0:T(8,128)(2,1)}, bf16[64,3584]{1,0:T(8,128)(2,1)S(1)}, u32[]{:S(2)}, u32[]{:S(2)}) collective-permute-start(bf16[64,3584]{1,0:T(8,128)(2,1)} %collective-permute-done.3), channel_id=1, source_target_pairs={{0,8},{8,0},{16,24},{24,16},{32,40},{40,32},{48,56},{56,48},{64,72... | collective-permute-start | bytes 1376264 | tf_op jit(solution)/shard_map/ppermute | solution.py:21
  86.7 17.1 %collective-permute-start.16 = (bf16[128,1024]{1,0:T(8,128)(2,1)S(1)}, bf16[128,1024]{1,0:T(8,128)(2,1)S(1)}, u32[]{:S(2)}, u32[]{:S(2)}) collective-permute-start(bf16[128,1024]{1,0:T(8,128)(2,1)S(1)} %get-tuple-element.110), channel_id=1, source_target_pairs={{0,16},{8,24},{16,32},{24,40},{32,48},{40,56},{48,64},{56,72},{64,... | collective-permute-start | bytes 786440 | tf_op jit(solution)/shard_map/ppermute | solution.py:17
  86.8 17.0 %collective-permute-start.17 = (bf16[128,1024]{1,0:T(8,128)(2,1)S(1)}, bf16[128,1024]{1,0:T(8,128)(2,1)S(1)}, u32[]{:S(2)}, u32[]{:S(2)}) collective-permute-start(bf16[128,1024]{1,0:T(8,128)(2,1)S(1)} %get-tuple-element.109), channel_id=1, source_target_pairs={{0,112},{8,120},{16,0},{24,8},{32,16},{40,24},{48,32},{56,40},{64,... | collective-permute-start | bytes 786440 | tf_op jit(solution)/shard_map/ppermute | solution.py:17
  90.9 13.0 %all-to-all-start.2 = ((bf16[8,32,896]{2,1,0:T(8,128)(2,1)}), bf16[8,32,896]{2,1,0:T(8,128)(2,1)S(1)}, u32[]{:S(2)}, u32[]{:S(2)}) async-start(bf16[8,32,896]{2,1,0:T(8,128)(2,1)} %broadcast_in_dim.22), calls=%async_computation.2 | async-start | bytes 917504 | tf_op jit(solution)/shard_map/all_to_all | solution.py:26
  95.7 14.1 %collective-permute-start.13 = (bf16[64,3584]{1,0:T(8,128)(2,1)}, bf16[64,3584]{1,0:T(8,128)(2,1)}, u32[]{:S(2)}, u32[]{:S(2)}) collective-permute-start(bf16[64,3584]{1,0:T(8,128)(2,1)} %collective-permute-done.8), channel_id=1, source_target_pairs={{0,16},{8,24},{16,32},{24,40},{32,48},{40,56},{48,64},{56,72},{64,... | collective-permute-start | bytes 1376264 | tf_op jit(solution)/shard_map/ppermute | solution.py:17
  95.7 14.1 %collective-permute-start.14 = (bf16[64,3584]{1,0:T(8,128)(2,1)}, bf16[64,3584]{1,0:T(8,128)(2,1)}, u32[]{:S(2)}, u32[]{:S(2)}) collective-permute-start(bf16[64,3584]{1,0:T(8,128)(2,1)} %collective-permute-done.10), channel_id=1, source_target_pairs={{0,112},{8,120},{16,0},{24,8},{32,16},{40,24},{48,32},{56,40},{64,... | collective-permute-start | bytes 1376264 | tf_op jit(solution)/shard_map/ppermute | solution.py:17
  110.9 22.8 %all-to-all-start.3 = ((f32[8,48,896]{2,1,0:T(8,128)}), f32[8,48,896]{2,1,0:T(8,128)S(1)}, u32[]{:S(2)}, u32[]{:S(2)}) async-start(f32[8,48,896]{2,1,0:T(8,128)} %bitcast.11), calls=%async_computation.3 | async-start | bytes 2752512 | tf_op jit(solution)/shard_map/all_to_all | solution.py:67
  117.1 17.4 %collective-permute-start.20 = (bf16[64,3584]{1,0:T(8,128)(2,1)}, bf16[64,3584]{1,0:T(8,128)(2,1)}, u32[]{:S(2)}, u32[]{:S(2)}) collective-permute-start(bf16[64,3584]{1,0:T(8,128)(2,1)} %collective-permute-done), channel_id=1, source_target_pairs={{0,8},{8,0},{16,24},{24,16},{32,40},{40,32},{48,56},{56,48},{64,72... | collective-permute-start | bytes 1376264 | tf_op jit(solution)/shard_map/ppermute | solution.py:21
  119.2 15.2 %collective-permute-start.21 = (bf16[128,1024]{1,0:T(8,128)(2,1)S(1)}, bf16[128,1024]{1,0:T(8,128)(2,1)S(1)}, u32[]{:S(2)}, u32[]{:S(2)}) collective-permute-start(bf16[128,1024]{1,0:T(8,128)(2,1)S(1)} %get-tuple-element.107), channel_id=1, source_target_pairs={{0,16},{8,24},{16,32},{24,40},{32,48},{40,56},{48,64},{56,72},{64,... | collective-permute-start | bytes 786440 | tf_op jit(solution)/shard_map/ppermute | solution.py:17
  119.6 19.0 %collective-permute-start.18 = (bf16[64,3584]{1,0:T(8,128)(2,1)}, bf16[64,3584]{1,0:T(8,128)(2,1)}, u32[]{:S(2)}, u32[]{:S(2)}) collective-permute-start(bf16[64,3584]{1,0:T(8,128)(2,1)} %copy-done.7), channel_id=1, source_target_pairs={{0,16},{8,24},{16,32},{24,40},{32,48},{40,56},{48,64},{56,72},{64,... | collective-permute-start | bytes 1376264 | tf_op jit(solution)/shard_map/ppermute | solution.py:17
  121.3 17.3 %collective-permute-start.19 = (bf16[64,3584]{1,0:T(8,128)(2,1)}, bf16[64,3584]{1,0:T(8,128)(2,1)}, u32[]{:S(2)}, u32[]{:S(2)}) collective-permute-start(bf16[64,3584]{1,0:T(8,128)(2,1)} %collective-permute-done.14), channel_id=1, source_target_pairs={{0,112},{8,120},{16,0},{24,8},{32,16},{40,24},{48,32},{56,40},{64,... | collective-permute-start | bytes 1376264 | tf_op jit(solution)/shard_map/ppermute | solution.py:17
  138.7 18.5 %collective-permute-start.22 = (f32[64,1024]{1,0:T(8,128)S(1)}, f32[64,1024]{1,0:T(8,128)S(1)}, u32[]{:S(2)}, u32[]{:S(2)}) collective-permute-start(f32[64,1024]{1,0:T(8,128)S(1)} %constant_dynamic-slice_fusion), channel_id=1, source_target_pairs={{0,8},{8,0},{16,24},{24,16},{32,40},{40,32},{48,56},{56,48},{64,72... | collective-permute-start | bytes 786440 | tf_op jit(solution)/shard_map/ppermute | solution.py:21
  181.0 25.0 %all-to-all-start.5 = ((bf16[8,48,896]{2,1,0:T(8,128)(2,1)}), bf16[8,48,896]{2,1,0:T(8,128)(2,1)}, u32[]{:S(2)}, u32[]{:S(2)}) async-start(bf16[8,48,896]{2,1,0:T(8,128)(2,1)} %broadcast_in_dim.24), calls=%async_computation.5 | async-start | bytes 1376256 | tf_op jit(solution)/shard_map/all_to_all | solution.py:26
  207.0 27.4 %all-to-all-start.6 = ((bf16[8,48,896]{2,1,0:T(8,128)(2,1)}), bf16[8,48,896]{2,1,0:T(8,128)(2,1)S(1)}, u32[]{:S(2)}, u32[]{:S(2)}) async-start(bf16[8,48,896]{2,1,0:T(8,128)(2,1)} %broadcast_in_dim.42), calls=%async_computation.6 | async-start | bytes 1376256 | tf_op jit(solution)/shard_map/all_to_all | solution.py:26
  211.8 22.6 %collective-permute-start.37 = (bf16[64,1024]{1,0:T(8,128)(2,1)S(1)}, bf16[64,1024]{1,0:T(8,128)(2,1)S(1)}, u32[]{:S(2)}, u32[]{:S(2)}) collective-permute-start(bf16[64,1024]{1,0:T(8,128)(2,1)S(1)} %collective-permute-done.23.refs_10_), channel_id=1, source_target_pairs={{0,8},{8,0},{16,24},{24,16},{32,40},{40,32},{48,56},{56,48},{64,72... | collective-permute-start | bytes 393224 | tf_op jit(solution)/shard_map/ppermute | solution.py:21
  217.5 13.6 %collective-permute-start.34 = (bf16[64,1024]{1,0:T(8,128)(2,1)S(1)}, bf16[64,1024]{1,0:T(8,128)(2,1)S(1)}, u32[]{:S(2)}, u32[]{:S(2)}) collective-permute-start(bf16[64,1024]{1,0:T(8,128)(2,1)S(1)} %collective-permute-done.26.refs_4_), channel_id=1, source_target_pairs={{0,8},{8,0},{16,24},{24,16},{32,40},{40,32},{48,56},{56,48},{64,72... | collective-permute-start | bytes 393224 | tf_op jit(solution)/shard_map/ppermute | solution.py:21
  222.6 8.5 %collective-permute-start.32 = (bf16[64,1024]{1,0:T(8,128)(2,1)S(1)}, bf16[64,1024]{1,0:T(8,128)(2,1)S(1)}, u32[]{:S(2)}, u32[]{:S(2)}) collective-permute-start(bf16[64,1024]{1,0:T(8,128)(2,1)S(1)} %collective-permute-done.29.refs_6_), channel_id=1, source_target_pairs={{0,16},{8,24},{16,32},{24,40},{32,48},{40,56},{48,64},{56,72},{64,... | collective-permute-start | bytes 393224 | tf_op jit(solution)/shard_map/ppermute | solution.py:17
  (21 other events, 177.5 us)

commit v2 on v0

v2 whole, which is shorter than its diff:
```python
import functools

import jax
import jax.numpy as jnp
from jax import lax
from jax.experimental import pallas as pl
from jax.experimental.pallas import tpu as pltpu
from jax.sharding import PartitionSpec as P

LEN = 128
SEQS = 8
HALF = LEN // 2
Z = 8
Y = 4
SEND = jnp.bfloat16
ALONG_Z = [[2 * z + h for z in range(Z)] for h in range(2)]
QUICK = pl.CostEstimate(flops=1, bytes_accessed=1, transcendentals=0)
VMEM_LIMIT = 48 * 2**20


def shift_z(x, step):
    pairs = [(z * 2 + h, (z + step) % Z * 2 + h) for z in range(Z) for h in range(2)]
    return lax.ppermute(x, "wide", pairs)


def swap_x(x):
    return lax.ppermute(x, "wide", [(i, i ^ 1) for i in range(2 * Z)])


def shift_y(x, step):
    pairs = [(y * 2 + c, (y + step) % Y * 2 + c) for y in range(Y) for c in range(2)]
    return lax.ppermute(x, "tp", pairs)


def swap_core(x):
    return lax.ppermute(x, "tp", [(i, i ^ 1) for i in range(2 * Y)])


def along_z(x):
    return lax.all_to_all(x, "wide", 0, 0, tiled=True, axis_index_groups=ALONG_Z)


def together(*values):
    return lax.optimization_barrier(values)


def rotate_kernel(count, core_ref, *refs):
    blocks, basis_ref = refs[:count], refs[count]
    mine_ref, theirs_ref, total = refs[count + 1 :]
    rows = jnp.concatenate([block[...] for block in blocks], axis=0)
    term = jnp.dot(rows, basis_ref[...], preferred_element_type=jnp.float32)

    @pl.when(pl.program_id(0) == 0)
    def _():
        total[...] = term

    @pl.when(pl.program_id(0) == 1)
    def _():
        total[...] += term
        half = count * HALF // 2
        core = core_ref[0]
        mine_ref[...] = total[pl.ds(pl.multiple_of(core * half, 16), half), :]
        theirs_ref[...] = total[pl.ds(pl.multiple_of((1 - core) * half, 16), half), :]


def rotate_in(blocks, basis, core):
    count = len(blocks)
    depth, cols = basis.shape
    tile = depth // 2
    half = count * HALF // 2
    shape = jax.ShapeDtypeStruct((half, cols), jnp.float32)
    whole = pl.BlockSpec((half, cols), lambda k, core: (0, 0))
    return pl.pallas_call(
        functools.partial(rotate_kernel, count),
        out_shape=(shape, shape),
        grid_spec=pltpu.PrefetchScalarGridSpec(
            num_scalar_prefetch=1,
            grid=(2,),
            in_specs=[pl.BlockSpec((HALF, tile), lambda k, core: (0, k))] * count
            + [pl.BlockSpec((tile, cols), lambda k, core: (k, 0))],
            out_specs=(whole, whole),
            scratch_shapes=[pltpu.VMEM((count * HALF, cols), jnp.float32)],
        ),
        compiler_params=pltpu.CompilerParams(vmem_limit_bytes=VMEM_LIMIT),
        cost_estimate=QUICK,
    )(core, *blocks, basis)


def partial_kernel(place_ref, *refs):
    grads, (near_ref, far_ref, out_ref) = refs[:4], refs[4:]
    y, core = place_ref[0], place_ref[1]
    rows = near_ref.shape[0]
    lefts = []
    for near, far in (grads[:2], grads[2:]):
        for k in range(Y):
            part = pl.ds(k * rows, rows)
            lefts.append(jnp.concatenate([near[part, :], far[part, :]], axis=0))
    left = jnp.concatenate(lefts, axis=1)
    right = jnp.concatenate([near_ref[...], far_ref[...]], axis=0)
    term = lax.dot_general(left, right, (((0,), (0,)), ((), ())), preferred_element_type=jnp.float32)
    for n in range(SEQS):
        owner = jnp.where(n < Y, core, 1 - core)
        sequence = 2 * lax.rem(y + n % Y, Y) + owner
        out_ref[sequence] = term[n * LEN : (n + 1) * LEN, :].astype(out_ref.dtype)


def partial_out(grads, near, far, place):
    cols = near.shape[1]
    vmem = pl.BlockSpec(memory_space=pltpu.VMEM)
    return pl.pallas_call(
        partial_kernel,
        out_shape=jax.ShapeDtypeStruct((SEQS, LEN, cols), SEND),
        in_specs=[pl.BlockSpec(memory_space=pltpu.SMEM)] + [vmem] * 6,
        out_specs=vmem,
        compiler_params=pltpu.CompilerParams(vmem_limit_bytes=VMEM_LIMIT),
        cost_estimate=QUICK,
    )(place, *grads, near, far)


def split_kernel(place_ref, mine_ref, got_ref, *outs):
    rows = outs[0].shape[0]
    place = place_ref[0]
    for k, out in enumerate(outs):
        start = pl.multiple_of(lax.rem(place + k, Y) * rows, 16)
        out[...] = mine_ref[pl.ds(start, rows), :] + got_ref[pl.ds(start, rows), :]


def split_sum(mine, got, place):
    half, cols = mine.shape
    shape = jax.ShapeDtypeStruct((half // Y, cols), jnp.float32)
    return pl.pallas_call(
        split_kernel,
        out_shape=(shape,) * Y,
        in_specs=[pl.BlockSpec(memory_space=pltpu.SMEM)] + [pl.BlockSpec(memory_space=pltpu.VMEM)] * 2,
        out_specs=(pl.BlockSpec(memory_space=pltpu.VMEM),) * Y,
        compiler_params=pltpu.CompilerParams(vmem_limit_bytes=VMEM_LIMIT),
    )(place, mine, got)


def join_kernel(place_ref, *refs):
    pieces, out = refs[:Y], refs[Y]
    rows = pieces[0].shape[0]
    for k, piece in enumerate(pieces):
        start = pl.multiple_of(lax.rem(place_ref[0] + k, Y) * rows, 16)
        out[pl.ds(start, rows), :] = piece[...]


def join(pieces, place):
    rows, cols = pieces[0].shape
    return pl.pallas_call(
        join_kernel,
        out_shape=jax.ShapeDtypeStruct((Y * rows, cols), pieces[0].dtype),
        in_specs=[pl.BlockSpec(memory_space=pltpu.SMEM)] + [pl.BlockSpec(memory_space=pltpu.VMEM)] * Y,
        out_specs=pl.BlockSpec(memory_space=pltpu.VMEM),
        compiler_params=pltpu.CompilerParams(vmem_limit_bytes=VMEM_LIMIT),
    )(place, *pieces)


def products_kernel(layout, place_ref, scale_ref, *refs):
    outs_ref, refs = refs[0], refs[1:]
    chunks = len(layout)
    halves, o_ref, rows = refs[: 2 * chunks], refs[-2], refs[-1]
    z, h, core = place_ref[0], place_ref[1], place_ref[2]

    @pl.when(pl.program_id(0) == 0)
    def _():
        for n, blocks in enumerate(layout):
            for other in range(2):
                source = halves[2 * n + other]
                first = core if other == 0 else 1 - core
                count = len(blocks) // 2
                for slot in range(count):
                    low, high = blocks[slot], blocks[count + slot]
                    index = jnp.where(first == 0, low[0], high[0])
                    side = jnp.where(first == 0, low[1], high[1])
                    half = jnp.where(side == 0, h, 1 - h)
                    start = pl.multiple_of(index * LEN + half * HALF, 16)
                    rows[pl.ds(start, HALF), :] = source[slot * HALF : (slot + 1) * HALF, :]

    total = None
    for n in range(SEQS):
        product = lax.dot_general(
            outs_ref[lax.rem(z + n, SEQS), 0],
            rows[n * LEN : (n + 1) * LEN, :],
            (((0,), (0,)), ((), ())),
            preferred_element_type=jnp.float32,
        )
        total = product * product if total is None else total + product * product
    o_ref[...] = total / scale_ref[0]


def products(rotated_out, chunks, layout, place, scale):
    _, _, _, half_cols = rotated_out.shape
    in_cols = chunks[0][0].shape[1]
    tile = 256
    per = half_cols // tile
    halves = [half for chunk in chunks for half in chunk]
    smem = pl.BlockSpec(memory_space=pltpu.SMEM)
    return pl.pallas_call(
        functools.partial(products_kernel, layout),
        out_shape=jax.ShapeDtypeStruct((2 * half_cols, in_cols), jnp.float32),
        grid=(2 * per,),
        in_specs=[smem, smem, pl.BlockSpec((SEQS, 1, LEN, tile), lambda i: (0, i // per, 0, i % per))]
        + [pl.BlockSpec(half.shape, lambda i: (0, 0)) for half in halves],
        out_specs=pl.BlockSpec((tile, in_cols), lambda i: (i, 0)),
        scratch_shapes=[pltpu.VMEM((SEQS * LEN, in_cols), jnp.bfloat16)],
        compiler_params=pltpu.CompilerParams(vmem_limit_bytes=VMEM_LIMIT),
        cost_estimate=QUICK,
    )(place, scale.reshape(1), rotated_out, *halves)


def scatter_y(mine, theirs, place):
    own, *away = split_sum(mine, swap_core(theirs), place)
    return own, [shift_y(piece, k + 1) for k, piece in enumerate(away)]


def gather_y(own, came, place):
    piece = (own + came[0] + came[1] + came[2]).astype(jnp.bfloat16)
    return join([piece] + [shift_y(piece, -k) for k in (1, 2, 3)], place)


def on_device(activations, grads_out, basis_in, basis_out, lengths):
    wide, tp = lax.axis_index("wide"), lax.axis_index("tp")
    z, h = wide // 2, wide % 2
    y, core = tp // 2, tp % 2
    place, core_at = y.reshape(1), core.reshape(1)
    rows, out_cols = basis_out.shape
    half_cols = out_cols // 2

    a, c = {}, {}
    a[0] = activations
    a[-1], a[1] = shift_z(a[0], 1), shift_z(a[0], -1)
    far = swap_x(lax.dynamic_slice(basis_out, (0, (1 - h) * half_cols), (rows, half_cols)))
    near = lax.dynamic_slice(basis_out, (0, h * half_cols), (rows, half_cols))
    grads = [grads_out] + [shift_y(grads_out, -k) for k in (1, 2, 3)]
    a[-1], a[1], near, far, *grads = together(a[-1], a[1], near, far, *grads)

    a[-2], a[2] = shift_z(a[-1], 1), shift_z(a[1], -1)
    grads_near = jnp.concatenate(grads, axis=0)
    grads_far = swap_x(grads_near)
    a[-2], a[2], grads_near, grads_far = together(a[-2], a[2], grads_near, grads_far)

    a[-3], a[3], c[2] = shift_z(a[-2], 1), shift_z(a[2], -1), swap_x(a[2])
    grads = [grads_near, grads_far, swap_core(grads_near), swap_core(grads_far)]
    part = partial_out(grads, near, far, jnp.stack([y, core]))
    a[-3], a[3], c[2], part, a[1], a[-2], a[-1], a[0], basis_in = together(
        a[-3], a[3], c[2], part, a[1], a[-2], a[-1], a[0], basis_in
    )

    first = [(0, 0), (1, 0), (2, 0), (3, 0), (-1, 0), (-2, 0), (-3, 0), (2, 1)]
    second = [(4, 0), (1, 1), (0, 1), (-2, 1), (-1, 1), (3, 1), (-3, 1), (4, 1)]
    block = lambda at: (a, c)[at[1]][at[0]]
    summands = along_z(part)
    a[4], c[3] = shift_z(a[-3], 1), shift_z(c[2], -1)
    c[-2], c[1], c[0], c[-1] = swap_x(a[-2]), swap_x(a[1]), swap_x(a[0]), swap_x(a[-1])
    c[-3], c[4] = shift_z(c[-2], 1), shift_z(c[3], -1)
    mine_a, theirs_a = rotate_in([block(at) for at in first], basis_in, core_at)
    a[4], c[-3], c[4], c[1], c[-1], c[0], summands, mine_a, theirs_a, basis_in = together(
        a[4], c[-3], c[4], c[1], c[-1], c[0], summands, mine_a, theirs_a, basis_in
    )

    token = lax.iota(jnp.int32, LEN)
    live = token < lax.dynamic_index_in_dim(lengths, z, 0, keepdims=False)
    summed = jnp.sum(summands.astype(jnp.float32), axis=0)
    summed = jnp.where(live[:, None], summed, 0.0).astype(jnp.bfloat16)
    copies = jnp.broadcast_to(summed[None], (2 * Z,) + summed.shape)
    copies, basis_in, theirs_a = together(copies, basis_in, theirs_a)
    rotated_out = lax.all_to_all(copies, "wide", 0, 0, tiled=True)
    own_a, came_a = scatter_y(mine_a, theirs_a, place)

    mine_b, theirs_b = rotate_in([block(at) for at in second], basis_in, core_at)
    own_b, came_b = scatter_y(mine_b, theirs_b, place)
    rows_a = gather_y(own_a, came_a, place)
    chunk_a = (rows_a, swap_core(rows_a))
    rows_b = gather_y(own_b, came_b, place)
    chunk_b = (rows_b, swap_core(rows_b))
    scale = jnp.sum(lengths).astype(jnp.float32)
    layout = [[(k % SEQS, side) for k, side in blocks] for blocks in (first, second)]
    rotated_out = rotated_out.reshape(SEQS, 2, LEN, half_cols)
    return products(rotated_out, [chunk_a, chunk_b], layout, jnp.stack([z, h, core]), scale)


def solution(mesh):
    placed = (
        P(("layer", "wide"), "tp"),
        P(("layer", "wide"), "tp"),
        P(("layer", "tp"), "wide"),
        P(("layer", "wide"), "tp"),
        P(),
    )
    return jax.shard_map(
        on_device, mesh=mesh, in_specs=placed, out_specs=P(("layer", "tp"), "wide"), check_vma=False
    )
```

time: 359 us -> 176 us (0.49)
  the two profiles are of different devices: /device:TPU:6 before, /device:TPU:8 now
where the time goes in v2:
time: 176 us; the launch traced here: 175 us
  starting transfers between devices  71.8 us (41%)
  waiting for transfers between devices  70.6 us (40%)
  Pallas kernels  24.2 us (14%)
  local copies, waits for them, and re-layouts  4.45 us (3%)
  other arithmetic  3.09 us (2%)
    ppermute x10, waiting for transfers between devices, shift_z(): return lax.ppermute(x, 'wide', pairs)  33.6 us
    ppermute x15, starting transfers between devices, shift_y(): return lax.ppermute(x, 'tp', pairs)  25.9 us
    ppermute x15, waiting for transfers between devices, shift_y(): return lax.ppermute(x, 'tp', pairs)  20.3 us
    ppermute x10, starting transfers between devices, shift_z(): return lax.ppermute(x, 'wide', pairs)  18.4 us
    pallas_call x2, Pallas kernels, rotate_in(): pl.pallas_call(functools.partial(rotate_kernel, count), out_shape=(shape,...  14.2 us
    ppermute x7, starting transfers between devices, swap_x(): return lax.ppermute(x, 'wide', [(i, i ^ 1) for i in range(2 * Z)])  13.6 us
    ppermute x7, waiting for transfers between devices, swap_x(): return lax.ppermute(x, 'wide', [(i, i ^ 1) for i in range(2 * Z)])  9.95 us
    all_to_all x1, starting transfers between devices, on_device(): rotated_out = lax.all_to_all(copies, 'wide', 0, 0, tiled=True)  7.47 us
  transfers between devices with their start and end apart: 40, of which 21 were waited for; matrix products, arithmetic and copies ran while one was open for 1% of the time, Pallas kernels for 10%

profile of v2, /device:TPU:8, one launch (start us, length us, event | category | flops | bytes accessed | tf_op | source)
XLA Modules:
  0.0 175.2 jit_solution(16808861363020739424)
XLA Ops:
  1.3 3.1 %collective-permute-start.2 = (bf16[512,512]{1,0:T(8,128)(2,1)S(1)}, bf16[512,512]{1,0:T(8,128)(2,1)S(1)}, u32[]{:S(2)}, u32[]{:S(2)}) collective-permute-start(bf16[512,512]{1,0:T(8,128)(2,1)S(1)} %get-tuple-element.97), channel_id=1, source_target_pairs={{0,8},{8,0},{16,24},{24,16},{32,40},{40,32},{48,56},{56,48},{64,72... | collective-permute-start | bytes 1572872 | tf_op jit(solution)/shard_map/ppermute | solution.py:27
  4.5 1.9 %collective-permute-start = (bf16[64,3584]{1,0:T(8,128)(2,1)S(1)}, bf16[64,3584]{1,0:T(8,128)(2,1)S(1)}, u32[]{:S(2)}, u32[]{:S(2)}) collective-permute-start(bf16[64,3584]{1,0:T(8,128)(2,1)S(1)} %copy-done), channel_id=1, source_target_pairs={{0,16},{8,24},{16,32},{24,40},{32,48},{40,56},{48,64},{56,72},{64,... | collective-permute-start | bytes 1376264 | tf_op jit(solution)/shard_map/ppermute | solution.py:23
  6.4 3.9 %collective-permute-start.1 = (bf16[64,3584]{1,0:T(8,128)(2,1)S(1)}, bf16[64,3584]{1,0:T(8,128)(2,1)S(1)}, u32[]{:S(2)}, u32[]{:S(2)}) collective-permute-start(bf16[64,3584]{1,0:T(8,128)(2,1)S(1)} %copy-done), channel_id=1, source_target_pairs={{0,112},{8,120},{16,0},{24,8},{32,16},{40,24},{48,32},{56,40},{64,... | collective-permute-start | bytes 1376264 | tf_op jit(solution)/shard_map/ppermute | solution.py:23
  10.8 2.6 %collective-permute-start.4 = (bf16[512,128]{1,0:T(8,128)(2,1)S(1)}, bf16[512,128]{1,0:T(8,128)(2,1)S(1)}, u32[]{:S(2)}, u32[]{:S(2)}) collective-permute-start(bf16[512,128]{1,0:T(8,128)(2,1)S(1)} %copy-done.10), channel_id=1, source_target_pairs={{0,4},{1,5},{2,6},{3,7},{4,0},{5,1},{6,2},{7,3},{8,12},{9,13},{10,... | collective-permute-start | bytes 393224 | tf_op jit(solution)/shard_map/ppermute | solution.py:32
  13.4 3.0 %collective-permute-done.3 = bf16[512,128]{1,0:T(8,128)(2,1)S(1)} collective-permute-done((bf16[512,128]{1,0:T(8,128)(2,1)S(1)}, bf16[512,128]{1,0:T(8,128)(2,1)S(1)}, u32[]{:S(2)}, u32[]{:S(2)}) %collective-permute-start.3) | collective-permute-done | bytes 131104 | tf_op jit(solution)/shard_map/ppermute | solution.py:32
  18.8 2.9 %collective-permute-done.5 = bf16[512,128]{1,0:T(8,128)(2,1)S(1)} collective-permute-done((bf16[512,128]{1,0:T(8,128)(2,1)S(1)}, bf16[512,128]{1,0:T(8,128)(2,1)S(1)}, u32[]{:S(2)}, u32[]{:S(2)}) %collective-permute-start.5) | collective-permute-done | bytes 131104 | tf_op jit(solution)/shard_map/ppermute | solution.py:32
  22.5 3.2 %collective-permute-start.7 = (bf16[64,3584]{1,0:T(8,128)(2,1)S(1)}, bf16[64,3584]{1,0:T(8,128)(2,1)}, u32[]{:S(2)}, u32[]{:S(2)}) collective-permute-start(bf16[64,3584]{1,0:T(8,128)(2,1)S(1)} %collective-permute-done.1.refs_1_), channel_id=1, source_target_pairs={{0,112},{8,120},{16,0},{24,8},{32,16},{40,24},{48,32},{56,40},{64,... | collective-permute-start | bytes 1376264 | tf_op jit(solution)/shard_map/ppermute | solution.py:23
  25.7 9.4 %collective-permute-done.6.refs_5_ = bf16[64,3584]{1,0:T(8,128)(2,1)} collective-permute-done((bf16[64,3584]{1,0:T(8,128)(2,1)S(1)}, bf16[64,3584]{1,0:T(8,128)(2,1)}, u32[]{:S(2)}, u32[]{:S(2)}) %collective-permute-start.6) | collective-permute-done | bytes 458784 | tf_op jit(solution)/shard_map/ppermute | solution.py:23
  35.7 2.9 %collective-permute-start.10 = (bf16[64,3584]{1,0:T(8,128)(2,1)}, bf16[64,3584]{1,0:T(8,128)(2,1)}, u32[]{:S(2)}, u32[]{:S(2)}) collective-permute-start(bf16[64,3584]{1,0:T(8,128)(2,1)} %collective-permute-done.7.refs_2_), channel_id=1, source_target_pairs={{0,112},{8,120},{16,0},{24,8},{32,16},{40,24},{48,32},{56,40},{64,... | collective-permute-start | bytes 1376264 | tf_op jit(solution)/shard_map/ppermute | solution.py:23
  40.6 2.8 %shard_map.55 = bf16[8,128,512]{2,1,0:T(8,128)(2,1)} custom-call(s32[2]{0:T(128)S(1)} %pad_add_fusion.1.place_ref, bf16[2048,128]{1,0:T(8,128)(2,1)S(1)} %constant_dynamic-update-slice_fusion.refs_0_, bf16[2048,128]{1,0:T(8,128)(2,1)S(1)} %collective-permute-done.8.refs_1_, bf16[2048,128]{1,0:T(8,128)(2,1)S(1)} %collective-permute-done.12.refs_2_, ...), custom_call_target="tpu_custom_call" | custom-call | flops 1 | bytes 1 | tf_op jit(solution)/shard_map/pallas_call | solution.py:110
  43.4 5.6 %collective-permute-done.10.refs_3_ = bf16[64,3584]{1,0:T(8,128)(2,1)} collective-permute-done((bf16[64,3584]{1,0:T(8,128)(2,1)}, bf16[64,3584]{1,0:T(8,128)(2,1)}, u32[]{:S(2)}, u32[]{:S(2)}) %collective-permute-start.10) | collective-permute-done | bytes 458784 | tf_op jit(solution)/shard_map/ppermute | solution.py:23
  49.0 3.7 %collective-permute-done.11.refs_7_ = bf16[64,3584]{1,0:T(8,128)(2,1)} collective-permute-done((bf16[64,3584]{1,0:T(8,128)(2,1)}, bf16[64,3584]{1,0:T(8,128)(2,1)}, u32[]{:S(2)}, u32[]{:S(2)}) %collective-permute-start.11) | collective-permute-done | bytes 458784 | tf_op jit(solution)/shard_map/ppermute | solution.py:27
  54.0 5.0 %all-to-all-start = ((bf16[8,128,512]{2,1,0:T(8,128)(2,1)}), bf16[8,128,512]{2,1,0:T(8,128)(2,1)}, u32[]{:S(2)}, u32[]{:S(2)}) async-start(bf16[8,128,512]{2,1,0:T(8,128)(2,1)} %shard_map.55), calls=%async_computation | async-start | bytes 2097152 | tf_op jit(solution)/shard_map/all_to_all | solution.py:40
  58.9 2.3 %collective-permute-start.15 = (bf16[64,3584]{1,0:T(8,128)(2,1)}, bf16[64,3584]{1,0:T(8,128)(2,1)}, u32[]{:S(2)}, u32[]{:S(2)}) collective-permute-start(bf16[64,3584]{1,0:T(8,128)(2,1)} %collective-permute-done.6.refs_5_), channel_id=1, source_target_pairs={{0,8},{8,0},{16,24},{24,16},{32,40},{40,32},{48,56},{56,48},{64,72... | collective-permute-start | bytes 1376264 | tf_op jit(solution)/shard_map/ppermute | solution.py:27
  61.2 3.2 %collective-permute-start.17 = (bf16[64,3584]{1,0:T(8,128)(2,1)}, bf16[64,3584]{1,0:T(8,128)(2,1)}, u32[]{:S(2)}, u32[]{:S(2)}) collective-permute-start(bf16[64,3584]{1,0:T(8,128)(2,1)} %collective-permute-done.11.refs_7_), channel_id=1, source_target_pairs={{0,112},{8,120},{16,0},{24,8},{32,16},{40,24},{48,32},{56,40},{64,... | collective-permute-start | bytes 1376264 | tf_op jit(solution)/shard_map/ppermute | solution.py:23
  65.7 2.3 %collective-permute-start.20 = (bf16[64,3584]{1,0:T(8,128)(2,1)}, bf16[64,3584]{1,0:T(8,128)(2,1)}, u32[]{:S(2)}, u32[]{:S(2)}) collective-permute-start(bf16[64,3584]{1,0:T(8,128)(2,1)} %copy-done.2), channel_id=1, source_target_pairs={{0,8},{8,0},{16,24},{24,16},{32,40},{40,32},{48,56},{56,48},{64,72... | collective-permute-start | bytes 1376264 | tf_op jit(solution)/shard_map/ppermute | solution.py:27
  68.0 6.2 %collective-permute-done.15.refs_3_ = bf16[64,3584]{1,0:T(8,128)(2,1)} collective-permute-done((bf16[64,3584]{1,0:T(8,128)(2,1)}, bf16[64,3584]{1,0:T(8,128)(2,1)}, u32[]{:S(2)}, u32[]{:S(2)}) %collective-permute-start.15) | collective-permute-done | bytes 458784 | tf_op jit(solution)/shard_map/ppermute | solution.py:27
  74.2 2.3 %collective-permute-start.21 = (bf16[64,3584]{1,0:T(8,128)(2,1)}, bf16[64,3584]{1,0:T(8,128)(2,1)}, u32[]{:S(2)}, u32[]{:S(2)}) collective-permute-start(bf16[64,3584]{1,0:T(8,128)(2,1)} %refs_0_), channel_id=1, source_target_pairs={{0,8},{8,0},{16,24},{24,16},{32,40},{40,32},{48,56},{56,48},{64,72... | collective-permute-start | bytes 1376264 | tf_op jit(solution)/shard_map/ppermute | solution.py:27
  76.5 16.0 %collective-permute-done.17.refs_5_ = bf16[64,3584]{1,0:T(8,128)(2,1)} collective-permute-done((bf16[64,3584]{1,0:T(8,128)(2,1)}, bf16[64,3584]{1,0:T(8,128)(2,1)}, u32[]{:S(2)}, u32[]{:S(2)}) %collective-permute-start.17) | collective-permute-done | bytes 458784 | tf_op jit(solution)/shard_map/ppermute | solution.py:23
  97.9 7.0 %shard_map.56 = (f32[256,896]{1,0:T(8,128)S(1)}, f32[256,896]{1,0:T(8,128)S(1)}) custom-call(s32[1]{0:T(128)} %bitcast.2.core_ref, bf16[64,3584]{1,0:T(8,128)(2,1)S(1)} %copy-done.1, bf16[64,3584]{1,0:T(8,128)(2,1)S(1)} %copy-done.5, bf16[64,3584]{1,0:T(8,128)(2,1)} %collective-permute-done.7.refs_2_, bf16[64,3584]{1,0:T(8,128)(2,1)} %collective-permute-done.10.refs_3_, ...), custom_call_target="tpu_custom_call" | custom-call | flops 1 | bytes 1 | tf_op jit(solution)/shard_map/pallas_call | solution.py:73
  109.3 7.5 %all-to-all-start.1 = ((bf16[16,128,512]{2,1,0:T(8,128)(2,1)}), bf16[16,128,512]{2,1,0:T(8,128)(2,1)S(1)}, u32[]{:S(2)}, u32[]{:S(2)}) async-start(bf16[16,128,512]{2,1,0:T(8,128)(2,1)} %broadcast_in_dim.21), calls=%async_computation.1 | async-start | bytes 4194304 | tf_op jit(solution)/shard_map/all_to_all | solution.py:268
  116.8 7.2 %shard_map.59 = (f32[256,896]{1,0:T(8,128)S(1)}, f32[256,896]{1,0:T(8,128)S(1)}) custom-call(s32[1]{0:T(128)} %bitcast.2.core_ref, bf16[64,3584]{1,0:T(8,128)(2,1)S(1)} %copy-done.7, bf16[64,3584]{1,0:T(8,128)(2,1)} %collective-permute-done.19.refs_1_, bf16[64,3584]{1,0:T(8,128)(2,1)} %collective-permute-done.21.refs_2_, ...), custom_call_target="tpu_custom_call" | custom-call | flops 1 | bytes 1 | tf_op jit(solution)/shard_map/pallas_call | solution.py:73
  124.6 2.0 %collective-permute-done.30.got_ref = f32[256,896]{1,0:T(8,128)S(1)} collective-permute-done((f32[256,896]{1,0:T(8,128)S(1)}, f32[256,896]{1,0:T(8,128)S(1)}, u32[]{:S(2)}, u32[]{:S(2)}) %collective-permute-start.30) | collective-permute-done | bytes 917536 | tf_op jit(solution)/shard_map/ppermute | solution.py:36
  128.3 2.0 %collective-permute-start.32 = (f32[64,896]{1,0:T(8,128)S(1)}, f32[64,896]{1,0:T(8,128)S(1)}, u32[]{:S(2)}, u32[]{:S(2)}) collective-permute-start(f32[64,896]{1,0:T(8,128)S(1)} %get-tuple-element.95), channel_id=1, source_target_pairs={{0,4},{1,5},{2,6},{3,7},{4,0},{5,1},{6,2},{7,3},{8,12},{9,13},{10,... | collective-permute-start | bytes 688136 | tf_op jit(solution)/shard_map/ppermute | solution.py:32
  132.5 2.8 %collective-permute-start.24 = (f32[64,896]{1,0:T(8,128)S(1)}, f32[64,896]{1,0:T(8,128)S(1)}, u32[]{:S(2)}, u32[]{:S(2)}) collective-permute-start(f32[64,896]{1,0:T(8,128)S(1)} %get-tuple-element.82), channel_id=1, source_target_pairs={{0,4},{1,5},{2,6},{3,7},{4,0},{5,1},{6,2},{7,3},{8,12},{9,13},{10,... | collective-permute-start | bytes 688136 | tf_op jit(solution)/shard_map/ppermute | solution.py:32
  135.2 3.5 %collective-permute-done.31 = f32[64,896]{1,0:T(8,128)S(1)} collective-permute-done((f32[64,896]{1,0:T(8,128)S(1)}, f32[64,896]{1,0:T(8,128)S(1)}, u32[]{:S(2)}, u32[]{:S(2)}) %collective-permute-start.31) | collective-permute-done | bytes 229408 | tf_op jit(solution)/shard_map/ppermute | solution.py:32
  138.7 3.6 %collective-permute-start.25 = (f32[64,896]{1,0:T(8,128)S(1)}, f32[64,896]{1,0:T(8,128)S(1)}, u32[]{:S(2)}, u32[]{:S(2)}) collective-permute-start(f32[64,896]{1,0:T(8,128)S(1)} %get-tuple-element.83), channel_id=1, source_target_pairs={{0,6},{1,7},{2,0},{3,1},{4,2},{5,3},{6,4},{7,5},{8,14},{9,15},{10,... | collective-permute-start | bytes 688136 | tf_op jit(solution)/shard_map/ppermute | solution.py:32
  145.5 2.5 %collective-permute-start.36 = (bf16[64,896]{1,0:T(8,128)(2,1)S(1)}, bf16[64,896]{1,0:T(8,128)(2,1)S(1)}, u32[]{:S(2)}, u32[]{:S(2)}) collective-permute-start(bf16[64,896]{1,0:T(8,128)(2,1)S(1)} %add_convert_fusion.refs_0_), channel_id=1, source_target_pairs={{0,2},{1,3},{2,4},{3,5},{4,6},{5,7},{6,0},{7,1},{8,10},{9,11},{10,... | collective-permute-start | bytes 344072 | tf_op jit(solution)/shard_map/ppermute | solution.py:32
  148.2 3.8 %collective-permute-done.25 = f32[64,896]{1,0:T(8,128)S(1)} collective-permute-done((f32[64,896]{1,0:T(8,128)S(1)}, f32[64,896]{1,0:T(8,128)S(1)}, u32[]{:S(2)}, u32[]{:S(2)}) %collective-permute-start.25) | collective-permute-done | bytes 229408 | tf_op jit(solution)/shard_map/ppermute | solution.py:32
  158.2 2.1 %collective-permute-done.26.refs_1_ = bf16[64,896]{1,0:T(8,128)(2,1)S(1)} collective-permute-done((bf16[64,896]{1,0:T(8,128)(2,1)S(1)}, bf16[64,896]{1,0:T(8,128)(2,1)S(1)}, u32[]{:S(2)}, u32[]{:S(2)}) %collective-permute-start.26) | collective-permute-done | bytes 114720 | tf_op jit(solution)/shard_map/ppermute | solution.py:32
  163.9 4.3 %all-to-all-done.1 = bf16[16,128,512]{2,1,0:T(8,128)(2,1)S(1)} async-done(((bf16[16,128,512]{2,1,0:T(8,128)(2,1)}), bf16[16,128,512]{2,1,0:T(8,128)(2,1)S(1)}, u32[]{:S(2)}, u32[]{:S(2)}) %all-to-all-start.1) | async-done | bytes 2097184 | tf_op jit(solution)/shard_map/all_to_all | solution.py:268
  168.2 7.0 %shard_map.62 = f32[1024,896]{1,0:T(8,128)} custom-call(s32[3]{0:T(128)S(1)} %pad_add_fusion.place_ref, f32[1]{0:T(128)} %bitcast.3.scale_ref, bf16[8,2,128,512]{3,2,1,0:T(8,128)(2,1)S(1)} %bitcast.7, bf16[256,896]{1,0:T(8,128)(2,1)S(1)} %shard_map.58.refs_1_, bf16[256,896]{1,0:T(8,128)(2,1)} %collective-permute-done.29.refs_2_, ...), custom_call_target="tpu_custom_call" | custom-call | flops 1 | bytes 1 | tf_op jit(solution)/shard_map/pallas_call | solution.py:199
  (95 shorter events, 36.7 us)
Async XLA Ops:
  1.3 20.4 %collective-permute-start.2 = (bf16[512,512]{1,0:T(8,128)(2,1)S(1)}, bf16[512,512]{1,0:T(8,128)(2,1)S(1)}, u32[]{:S(2)}, u32[]{:S(2)}) collective-permute-start(bf16[512,512]{1,0:T(8,128)(2,1)S(1)} %get-tuple-element.97), channel_id=1, source_target_pairs={{0,8},{8,0},{16,24},{24,16},{32,40},{40,32},{48,56},{56,48},{64,72... | collective-permute-start | bytes 1572872 | tf_op jit(solution)/shard_map/ppermute | solution.py:27
  4.5 17.3 %collective-permute-start = (bf16[64,3584]{1,0:T(8,128)(2,1)S(1)}, bf16[64,3584]{1,0:T(8,128)(2,1)S(1)}, u32[]{:S(2)}, u32[]{:S(2)}) collective-permute-start(bf16[64,3584]{1,0:T(8,128)(2,1)S(1)} %copy-done), channel_id=1, source_target_pairs={{0,16},{8,24},{16,32},{24,40},{32,48},{40,56},{48,64},{56,72},{64,... | collective-permute-start | bytes 1376264 | tf_op jit(solution)/shard_map/ppermute | solution.py:23
  6.4 15.4 %collective-permute-start.1 = (bf16[64,3584]{1,0:T(8,128)(2,1)S(1)}, bf16[64,3584]{1,0:T(8,128)(2,1)S(1)}, u32[]{:S(2)}, u32[]{:S(2)}) collective-permute-start(bf16[64,3584]{1,0:T(8,128)(2,1)S(1)} %copy-done), channel_id=1, source_target_pairs={{0,112},{8,120},{16,0},{24,8},{32,16},{40,24},{48,32},{56,40},{64,... | collective-permute-start | bytes 1376264 | tf_op jit(solution)/shard_map/ppermute | solution.py:23
  10.8 8.0 %collective-permute-start.4 = (bf16[512,128]{1,0:T(8,128)(2,1)S(1)}, bf16[512,128]{1,0:T(8,128)(2,1)S(1)}, u32[]{:S(2)}, u32[]{:S(2)}) collective-permute-start(bf16[512,128]{1,0:T(8,128)(2,1)S(1)} %copy-done.10), channel_id=1, source_target_pairs={{0,4},{1,5},{2,6},{3,7},{4,0},{5,1},{6,2},{7,3},{8,12},{9,13},{10,... | collective-permute-start | bytes 393224 | tf_op jit(solution)/shard_map/ppermute | solution.py:32
  21.9 13.2 %collective-permute-start.8 = (bf16[2048,128]{1,0:T(8,128)(2,1)S(1)}, bf16[2048,128]{1,0:T(8,128)(2,1)S(1)}, u32[]{:S(2)}, u32[]{:S(2)}) collective-permute-start(bf16[2048,128]{1,0:T(8,128)(2,1)S(1)} %constant_dynamic-update-slice_fusion.refs_0_), channel_id=1, source_target_pairs={{0,8},{8,0},{16,24},{24,16},{32,40},{40,32},{48,56},{56,48},{64,72... | collective-permute-start | bytes 1572872 | tf_op jit(solution)/shard_map/ppermute | solution.py:27
  22.5 12.6 %collective-permute-start.6 = (bf16[64,3584]{1,0:T(8,128)(2,1)S(1)}, bf16[64,3584]{1,0:T(8,128)(2,1)}, u32[]{:S(2)}, u32[]{:S(2)}) collective-permute-start(bf16[64,3584]{1,0:T(8,128)(2,1)S(1)} %collective-permute-done.refs_4_), channel_id=1, source_target_pairs={{0,16},{8,24},{16,32},{24,40},{32,48},{40,56},{48,64},{56,72},{64,... | collective-permute-start | bytes 1376264 | tf_op jit(solution)/shard_map/ppermute | solution.py:23
  22.5 12.6 %collective-permute-start.7 = (bf16[64,3584]{1,0:T(8,128)(2,1)S(1)}, bf16[64,3584]{1,0:T(8,128)(2,1)}, u32[]{:S(2)}, u32[]{:S(2)}) collective-permute-start(bf16[64,3584]{1,0:T(8,128)(2,1)S(1)} %collective-permute-done.1.refs_1_), channel_id=1, source_target_pairs={{0,112},{8,120},{16,0},{24,8},{32,16},{40,24},{48,32},{56,40},{64,... | collective-permute-start | bytes 1376264 | tf_op jit(solution)/shard_map/ppermute | solution.py:23
  35.7 13.2 %collective-permute-start.10 = (bf16[64,3584]{1,0:T(8,128)(2,1)}, bf16[64,3584]{1,0:T(8,128)(2,1)}, u32[]{:S(2)}, u32[]{:S(2)}) collective-permute-start(bf16[64,3584]{1,0:T(8,128)(2,1)} %collective-permute-done.7.refs_2_), channel_id=1, source_target_pairs={{0,112},{8,120},{16,0},{24,8},{32,16},{40,24},{48,32},{56,40},{64,... | collective-permute-start | bytes 1376264 | tf_op jit(solution)/shard_map/ppermute | solution.py:23
  38.6 14.1 %collective-permute-start.11 = (bf16[64,3584]{1,0:T(8,128)(2,1)}, bf16[64,3584]{1,0:T(8,128)(2,1)}, u32[]{:S(2)}, u32[]{:S(2)}) collective-permute-start(bf16[64,3584]{1,0:T(8,128)(2,1)} %collective-permute-done.7.refs_2_), channel_id=1, source_target_pairs={{0,8},{8,0},{16,24},{24,16},{32,40},{40,32},{48,56},{56,48},{64,72... | collective-permute-start | bytes 1376264 | tf_op jit(solution)/shard_map/ppermute | solution.py:27
  40.5 13.5 %collective-permute-start.9 = (bf16[64,3584]{1,0:T(8,128)(2,1)}, bf16[64,3584]{1,0:T(8,128)(2,1)}, u32[]{:S(2)}, u32[]{:S(2)}) collective-permute-start(bf16[64,3584]{1,0:T(8,128)(2,1)} %collective-permute-done.6.refs_5_), channel_id=1, source_target_pairs={{0,16},{8,24},{16,32},{24,40},{32,48},{40,56},{48,64},{56,72},{64,... | collective-permute-start | bytes 1376264 | tf_op jit(solution)/shard_map/ppermute | solution.py:23
  54.0 52.3 %all-to-all-start = ((bf16[8,128,512]{2,1,0:T(8,128)(2,1)}), bf16[8,128,512]{2,1,0:T(8,128)(2,1)}, u32[]{:S(2)}, u32[]{:S(2)}) async-start(bf16[8,128,512]{2,1,0:T(8,128)(2,1)} %shard_map.55), calls=%async_computation | async-start | bytes 2097152 | tf_op jit(solution)/shard_map/all_to_all | solution.py:40
  58.9 15.3 %collective-permute-start.15 = (bf16[64,3584]{1,0:T(8,128)(2,1)}, bf16[64,3584]{1,0:T(8,128)(2,1)}, u32[]{:S(2)}, u32[]{:S(2)}) collective-permute-start(bf16[64,3584]{1,0:T(8,128)(2,1)} %collective-permute-done.6.refs_5_), channel_id=1, source_target_pairs={{0,8},{8,0},{16,24},{24,16},{32,40},{40,32},{48,56},{56,48},{64,72... | collective-permute-start | bytes 1376264 | tf_op jit(solution)/shard_map/ppermute | solution.py:27
  61.2 31.3 %collective-permute-start.17 = (bf16[64,3584]{1,0:T(8,128)(2,1)}, bf16[64,3584]{1,0:T(8,128)(2,1)}, u32[]{:S(2)}, u32[]{:S(2)}) collective-permute-start(bf16[64,3584]{1,0:T(8,128)(2,1)} %collective-permute-done.11.refs_7_), channel_id=1, source_target_pairs={{0,112},{8,120},{16,0},{24,8},{32,16},{40,24},{48,32},{56,40},{64,... | collective-permute-start | bytes 1376264 | tf_op jit(solution)/shard_map/ppermute | solution.py:23
  64.4 29.5 %collective-permute-start.14 = (bf16[64,3584]{1,0:T(8,128)(2,1)}, bf16[64,3584]{1,0:T(8,128)(2,1)S(1)}, u32[]{:S(2)}, u32[]{:S(2)}) collective-permute-start(bf16[64,3584]{1,0:T(8,128)(2,1)} %collective-permute-done.9.refs_6_), channel_id=1, source_target_pairs={{0,16},{8,24},{16,32},{24,40},{32,48},{40,56},{48,64},{56,72},{64,... | collective-permute-start | bytes 1376264 | tf_op jit(solution)/shard_map/ppermute | solution.py:23
  64.4 40.5 %collective-permute-start.19 = (bf16[64,3584]{1,0:T(8,128)(2,1)}, bf16[64,3584]{1,0:T(8,128)(2,1)}, u32[]{:S(2)}, u32[]{:S(2)}) collective-permute-start(bf16[64,3584]{1,0:T(8,128)(2,1)} %copy-done.4), channel_id=1, source_target_pairs={{0,8},{8,0},{16,24},{24,16},{32,40},{40,32},{48,56},{56,48},{64,72... | collective-permute-start | bytes 1376264 | tf_op jit(solution)/shard_map/ppermute | solution.py:27
  65.7 39.3 %collective-permute-start.20 = (bf16[64,3584]{1,0:T(8,128)(2,1)}, bf16[64,3584]{1,0:T(8,128)(2,1)}, u32[]{:S(2)}, u32[]{:S(2)}) collective-permute-start(bf16[64,3584]{1,0:T(8,128)(2,1)} %copy-done.2), channel_id=1, source_target_pairs={{0,8},{8,0},{16,24},{24,16},{32,40},{40,32},{48,56},{56,48},{64,72... | collective-permute-start | bytes 1376264 | tf_op jit(solution)/shard_map/ppermute | solution.py:27
  74.2 30.8 %collective-permute-start.21 = (bf16[64,3584]{1,0:T(8,128)(2,1)}, bf16[64,3584]{1,0:T(8,128)(2,1)}, u32[]{:S(2)}, u32[]{:S(2)}) collective-permute-start(bf16[64,3584]{1,0:T(8,128)(2,1)} %refs_0_), channel_id=1, source_target_pairs={{0,8},{8,0},{16,24},{24,16},{32,40},{40,32},{48,56},{56,48},{64,72... | collective-permute-start | bytes 1376264 | tf_op jit(solution)/shard_map/ppermute | solution.py:27
  92.5 12.5 %collective-permute-start.16 = (bf16[64,3584]{1,0:T(8,128)(2,1)}, bf16[64,3584]{1,0:T(8,128)(2,1)}, u32[]{:S(2)}, u32[]{:S(2)}) collective-permute-start(bf16[64,3584]{1,0:T(8,128)(2,1)} %collective-permute-done.15.refs_3_), channel_id=1, source_target_pairs={{0,16},{8,24},{16,32},{24,40},{32,48},{40,56},{48,64},{56,72},{64,... | collective-permute-start | bytes 1376264 | tf_op jit(solution)/shard_map/ppermute | solution.py:23
  94.8 11.5 %collective-permute-start.18 = (bf16[64,3584]{1,0:T(8,128)(2,1)}, bf16[64,3584]{1,0:T(8,128)(2,1)}, u32[]{:S(2)}, u32[]{:S(2)}) collective-permute-start(bf16[64,3584]{1,0:T(8,128)(2,1)} %collective-permute-done.17.refs_5_), channel_id=1, source_target_pairs={{0,112},{8,120},{16,0},{24,8},{32,16},{40,24},{48,32},{56,40},{64,... | collective-permute-start | bytes 1376264 | tf_op jit(solution)/shard_map/ppermute | solution.py:23
  109.3 58.9 %all-to-all-start.1 = ((bf16[16,128,512]{2,1,0:T(8,128)(2,1)}), bf16[16,128,512]{2,1,0:T(8,128)(2,1)S(1)}, u32[]{:S(2)}, u32[]{:S(2)}) async-start(bf16[16,128,512]{2,1,0:T(8,128)(2,1)} %broadcast_in_dim.21), calls=%async_computation.1 | async-start | bytes 4194304 | tf_op jit(solution)/shard_map/all_to_all | solution.py:268
  124.1 7.6 %collective-permute-start.22 = (f32[256,896]{1,0:T(8,128)S(1)}, f32[256,896]{1,0:T(8,128)S(1)}, u32[]{:S(2)}, u32[]{:S(2)}) collective-permute-start(f32[256,896]{1,0:T(8,128)S(1)} %copy-done.9), channel_id=1, source_target_pairs={{0,1},{1,0},{2,3},{3,2},{4,5},{5,4},{6,7},{7,6},{8,9},{9,8},{10,11... | collective-permute-start | bytes 2752520 | tf_op jit(solution)/shard_map/ppermute | solution.py:36
  126.6 12.1 %collective-permute-start.31 = (f32[64,896]{1,0:T(8,128)S(1)}, f32[64,896]{1,0:T(8,128)S(1)}, u32[]{:S(2)}, u32[]{:S(2)}) collective-permute-start(f32[64,896]{1,0:T(8,128)S(1)} %get-tuple-element.94), channel_id=1, source_target_pairs={{0,2},{1,3},{2,4},{3,5},{4,6},{5,7},{6,0},{7,1},{8,10},{9,11},{10,... | collective-permute-start | bytes 688136 | tf_op jit(solution)/shard_map/ppermute | solution.py:32
  128.3 14.0 %collective-permute-start.32 = (f32[64,896]{1,0:T(8,128)S(1)}, f32[64,896]{1,0:T(8,128)S(1)}, u32[]{:S(2)}, u32[]{:S(2)}) collective-permute-start(f32[64,896]{1,0:T(8,128)S(1)} %get-tuple-element.95), channel_id=1, source_target_pairs={{0,4},{1,5},{2,6},{3,7},{4,0},{5,1},{6,2},{7,3},{8,12},{9,13},{10,... | collective-permute-start | bytes 688136 | tf_op jit(solution)/shard_map/ppermute | solution.py:32
  130.3 13.0 %collective-permute-start.33 = (f32[64,896]{1,0:T(8,128)S(1)}, f32[64,896]{1,0:T(8,128)S(1)}, u32[]{:S(2)}, u32[]{:S(2)}) collective-permute-start(f32[64,896]{1,0:T(8,128)S(1)} %get-tuple-element.96), channel_id=1, source_target_pairs={{0,6},{1,7},{2,0},{3,1},{4,2},{5,3},{6,4},{7,5},{8,14},{9,15},{10,... | collective-permute-start | bytes 688136 | tf_op jit(solution)/shard_map/ppermute | solution.py:32
  131.8 13.7 %collective-permute-start.23 = (f32[64,896]{1,0:T(8,128)S(1)}, f32[64,896]{1,0:T(8,128)S(1)}, u32[]{:S(2)}, u32[]{:S(2)}) collective-permute-start(f32[64,896]{1,0:T(8,128)S(1)} %get-tuple-element.81), channel_id=1, source_target_pairs={{0,2},{1,3},{2,4},{3,5},{4,6},{5,7},{6,0},{7,1},{8,10},{9,11},{10,... | collective-permute-start | bytes 688136 | tf_op jit(solution)/shard_map/ppermute | solution.py:32
  132.5 15.7 %collective-permute-start.24 = (f32[64,896]{1,0:T(8,128)S(1)}, f32[64,896]{1,0:T(8,128)S(1)}, u32[]{:S(2)}, u32[]{:S(2)}) collective-permute-start(f32[64,896]{1,0:T(8,128)S(1)} %get-tuple-element.82), channel_id=1, source_target_pairs={{0,4},{1,5},{2,6},{3,7},{4,0},{5,1},{6,2},{7,3},{8,12},{9,13},{10,... | collective-permute-start | bytes 688136 | tf_op jit(solution)/shard_map/ppermute | solution.py:32
  138.7 13.3 %collective-permute-start.25 = (f32[64,896]{1,0:T(8,128)S(1)}, f32[64,896]{1,0:T(8,128)S(1)}, u32[]{:S(2)}, u32[]{:S(2)}) collective-permute-start(f32[64,896]{1,0:T(8,128)S(1)} %get-tuple-element.83), channel_id=1, source_target_pairs={{0,6},{1,7},{2,0},{3,1},{4,2},{5,3},{6,4},{7,5},{8,14},{9,15},{10,... | collective-permute-start | bytes 688136 | tf_op jit(solution)/shard_map/ppermute | solution.py:32
  143.4 12.2 %collective-permute-start.34 = (bf16[64,896]{1,0:T(8,128)(2,1)S(1)}, bf16[64,896]{1,0:T(8,128)(2,1)S(1)}, u32[]{:S(2)}, u32[]{:S(2)}) collective-permute-start(bf16[64,896]{1,0:T(8,128)(2,1)S(1)} %add_convert_fusion.refs_0_), channel_id=1, source_target_pairs={{0,6},{1,7},{2,0},{3,1},{4,2},{5,3},{6,4},{7,5},{8,14},{9,15},{10,... | collective-permute-start | bytes 344072 | tf_op jit(solution)/shard_map/ppermute | solution.py:32
  143.8 14.2 %collective-permute-start.35 = (bf16[64,896]{1,0:T(8,128)(2,1)S(1)}, bf16[64,896]{1,0:T(8,128)(2,1)S(1)}, u32[]{:S(2)}, u32[]{:S(2)}) collective-permute-start(bf16[64,896]{1,0:T(8,128)(2,1)S(1)} %add_convert_fusion.refs_0_), channel_id=1, source_target_pairs={{0,4},{1,5},{2,6},{3,7},{4,0},{5,1},{6,2},{7,3},{8,12},{9,13},{10,... | collective-permute-start | bytes 344072 | tf_op jit(solution)/shard_map/ppermute | solution.py:32
  145.5 12.5 %collective-permute-start.36 = (bf16[64,896]{1,0:T(8,128)(2,1)S(1)}, bf16[64,896]{1,0:T(8,128)(2,1)S(1)}, u32[]{:S(2)}, u32[]{:S(2)}) collective-permute-start(bf16[64,896]{1,0:T(8,128)(2,1)S(1)} %add_convert_fusion.refs_0_), channel_id=1, source_target_pairs={{0,2},{1,3},{2,4},{3,5},{4,6},{5,7},{6,0},{7,1},{8,10},{9,11},{10,... | collective-permute-start | bytes 344072 | tf_op jit(solution)/shard_map/ppermute | solution.py:32
  152.0 8.3 %collective-permute-start.26 = (bf16[64,896]{1,0:T(8,128)(2,1)S(1)}, bf16[64,896]{1,0:T(8,128)(2,1)S(1)}, u32[]{:S(2)}, u32[]{:S(2)}) collective-permute-start(bf16[64,896]{1,0:T(8,128)(2,1)S(1)} %add_convert_fusion.1.refs_0_), channel_id=1, source_target_pairs={{0,6},{1,7},{2,0},{3,1},{4,2},{5,3},{6,4},{7,5},{8,14},{9,15},{10,... | collective-permute-start | bytes 344072 | tf_op jit(solution)/shard_map/ppermute | solution.py:32
  153.7 8.1 %collective-permute-start.27 = (bf16[64,896]{1,0:T(8,128)(2,1)S(1)}, bf16[64,896]{1,0:T(8,128)(2,1)S(1)}, u32[]{:S(2)}, u32[]{:S(2)}) collective-permute-start(bf16[64,896]{1,0:T(8,128)(2,1)S(1)} %add_convert_fusion.1.refs_0_), channel_id=1, source_target_pairs={{0,4},{1,5},{2,6},{3,7},{4,0},{5,1},{6,2},{7,3},{8,12},{9,13},{10,... | collective-permute-start | bytes 344072 | tf_op jit(solution)/shard_map/ppermute | solution.py:32
  (20 other events, 316.8 us)

commit v3 on v2

--- a/solution.py
+++ b/solution.py
@@ -192,7 +192,7 @@
 def products(rotated_out, chunks, layout, place, scale):
     _, _, _, half_cols = rotated_out.shape
     in_cols = chunks[0][0].shape[1]
-    tile = 256
+    tile = 512
     per = half_cols // tile
     halves = [half for chunk in chunks for half in chunk]
     smem = pl.BlockSpec(memory_space=pltpu.SMEM)
@@ -252,20 +252,21 @@
     block = lambda at: (a, c)[at[1]][at[0]]
     summands = along_z(part)
     a[4], c[3] = shift_z(a[-3], 1), shift_z(c[2], -1)
-    c[-2], c[1], c[0], c[-1] = swap_x(a[-2]), swap_x(a[1]), swap_x(a[0]), swap_x(a[-1])
-    c[-3], c[4] = shift_z(c[-2], 1), shift_z(c[3], -1)
+    c[-2], c[1], c[0] = swap_x(a[-2]), swap_x(a[1]), swap_x(a[0])
     mine_a, theirs_a = rotate_in([block(at) for at in first], basis_in, core_at)
-    a[4], c[-3], c[4], c[1], c[-1], c[0], summands, mine_a, theirs_a, basis_in = together(
-        a[4], c[-3], c[4], c[1], c[-1], c[0], summands, mine_a, theirs_a, basis_in
-    )
-
+    a[4], c[3], c[-2], c[1], mine_a, theirs_a, a[-1], basis_in, lengths = together(
+        a[4], c[3], c[-2], c[1], mine_a, theirs_a, a[-1], basis_in, lengths
+    )
+
+    c[-3], c[4], c[-1] = shift_z(c[-2], 1), shift_z(c[3], -1), swap_x(a[-1])
     token = lax.iota(jnp.int32, LEN)
     live = token < lax.dynamic_index_in_dim(lengths, z, 0, keepdims=False)
     summed = jnp.sum(summands.astype(jnp.float32), axis=0)
     summed = jnp.where(live[:, None], summed, 0.0).astype(jnp.bfloat16)
     copies = jnp.broadcast_to(summed[None], (2 * Z,) + summed.shape)
-    copies, basis_in, theirs_a = together(copies, basis_in, theirs_a)
+    c[-3], c[4], c[-1], c[0], copies, theirs_a = together(c[-3], c[4], c[-1], c[0], copies, theirs_a)
     rotated_out = lax.all_to_all(copies, "wide", 0, 0, tiled=True)
+
     own_a, came_a = scatter_y(mine_a, theirs_a, place)
 
     mine_b, theirs_b = rotate_in([block(at) for at in second], basis_in, core_at)

time: 176 us -> 172 us (0.977)
  waiting for transfers between devices: 70.6 us -> 67.8 us
  local copies, waits for them, and re-layouts: 4.45 us -> 6.6 us
    ppermute x7, waiting for transfers between devices: 9.95 us -> 5.56 us  [swap_x(): return lax.ppermute(x, 'wide', [(i, i ^ 1) for i in range(2 * Z)])]
    ppermute x15, waiting for transfers between devices: 20.3 us -> 22.7 us  [shift_y(): return lax.ppermute(x, 'tp', pairs)]
    unnamed x27 -> x29, local copies, waits for them, and re-layouts: 0.91 us -> 3.05 us
    ppermute x10, waiting for transfers between devices: 33.6 us -> 35.6 us  [shift_z(): return lax.ppermute(x, 'wide', pairs)]
    ppermute x6, waiting for transfers between devices: 2.44 us -> 0.56 us  [swap_core(): return lax.ppermute(x, 'tp', [(i, i ^ 1) for i in range(2 * Y)])]
  transfers between devices with their start and end apart: 40 -> 40, of which waited for: 21 -> 19; matrix products, arithmetic and copies ran while one was open for 1% -> 2% of each run, Pallas kernels for 10% -> 10%
where the time goes in v3:
time: 172 us
  starting transfers between devices  70.1 us (41%)
  waiting for transfers between devices  67.8 us (39%)
  Pallas kernels  23.7 us (14%)
  local copies, waits for them, and re-layouts  6.6 us (4%)
  other arithmetic  2.98 us (2%)
    ppermute x10, waiting for transfers between devices, shift_z(): return lax.ppermute(x, 'wide', pairs)  35.6 us
    ppermute x15, starting transfers between devices, shift_y(): return lax.ppermute(x, 'tp', pairs)  24.9 us
    ppermute x15, waiting for transfers between devices, shift_y(): return lax.ppermute(x, 'tp', pairs)  22.7 us
    ppermute x10, starting transfers between devices, shift_z(): return lax.ppermute(x, 'wide', pairs)  17.4 us
    pallas_call x2, Pallas kernels, rotate_in(): pl.pallas_call(functools.partial(rotate_kernel, count), out_shape=(shape,...  14 us
    ppermute x7, starting transfers between devices, swap_x(): return lax.ppermute(x, 'wide', [(i, i ^ 1) for i in range(2 * Z)])  13.9 us
    pallas_call x1, Pallas kernels, products(): pl.pallas_call(functools.partial(products_kernel, layout), out_shape=jax....  6.73 us
    all_to_all x1, starting transfers between devices, on_device(): rotated_out = lax.all_to_all(copies, 'wide', 0, 0, tiled=True)  6.66 us
  transfers between devices with their start and end apart: 40, of which 19 were waited for; matrix products, arithmetic and copies ran while one was open for 2% of the time, Pallas kernels for 10%

profile of v3, /device:TPU:8, one launch (start us, length us, event | category | flops | bytes accessed | tf_op | source)
XLA Modules:
  0.0 172.1 jit_solution(11472647816157276058)
XLA Ops:
  1.3 3.1 %collective-permute-start.2 = (bf16[512,512]{1,0:T(8,128)(2,1)S(1)}, bf16[512,512]{1,0:T(8,128)(2,1)S(1)}, u32[]{:S(2)}, u32[]{:S(2)}) collective-permute-start(bf16[512,512]{1,0:T(8,128)(2,1)S(1)} %get-tuple-element.101), channel_id=1, source_target_pairs={{0,8},{8,0},{16,24},{24,16},{32,40},{40,32},{48,56},{56,48},{64,72... | collective-permute-start | bytes 1572872 | tf_op jit(solution)/shard_map/ppermute | solution.py:27
  4.5 1.9 %collective-permute-start = (bf16[64,3584]{1,0:T(8,128)(2,1)S(1)}, bf16[64,3584]{1,0:T(8,128)(2,1)S(1)}, u32[]{:S(2)}, u32[]{:S(2)}) collective-permute-start(bf16[64,3584]{1,0:T(8,128)(2,1)S(1)} %copy-done), channel_id=1, source_target_pairs={{0,16},{8,24},{16,32},{24,40},{32,48},{40,56},{48,64},{56,72},{64,... | collective-permute-start | bytes 1376264 | tf_op jit(solution)/shard_map/ppermute | solution.py:23
  6.4 3.9 %collective-permute-start.1 = (bf16[64,3584]{1,0:T(8,128)(2,1)S(1)}, bf16[64,3584]{1,0:T(8,128)(2,1)S(1)}, u32[]{:S(2)}, u32[]{:S(2)}) collective-permute-start(bf16[64,3584]{1,0:T(8,128)(2,1)S(1)} %copy-done), channel_id=1, source_target_pairs={{0,112},{8,120},{16,0},{24,8},{32,16},{40,24},{48,32},{56,40},{64,... | collective-permute-start | bytes 1376264 | tf_op jit(solution)/shard_map/ppermute | solution.py:23
  10.3 2.3 %collective-permute-start.4 = (bf16[512,128]{1,0:T(8,128)(2,1)S(1)}, bf16[512,128]{1,0:T(8,128)(2,1)S(1)}, u32[]{:S(2)}, u32[]{:S(2)}) collective-permute-start(bf16[512,128]{1,0:T(8,128)(2,1)S(1)} %copy-done.11), channel_id=1, source_target_pairs={{0,4},{1,5},{2,6},{3,7},{4,0},{5,1},{6,2},{7,3},{8,12},{9,13},{10,... | collective-permute-start | bytes 393224 | tf_op jit(solution)/shard_map/ppermute | solution.py:32
  14.0 4.0 %collective-permute-done.4 = bf16[512,128]{1,0:T(8,128)(2,1)S(1)} collective-permute-done((bf16[512,128]{1,0:T(8,128)(2,1)S(1)}, bf16[512,128]{1,0:T(8,128)(2,1)S(1)}, u32[]{:S(2)}, u32[]{:S(2)}) %collective-permute-start.4) | collective-permute-done | bytes 131104 | tf_op jit(solution)/shard_map/ppermute | solution.py:32
  19.3 3.6 %collective-permute-done.5 = bf16[512,128]{1,0:T(8,128)(2,1)S(1)} collective-permute-done((bf16[512,128]{1,0:T(8,128)(2,1)S(1)}, bf16[512,128]{1,0:T(8,128)(2,1)S(1)}, u32[]{:S(2)}, u32[]{:S(2)}) %collective-permute-start.5) | collective-permute-done | bytes 131104 | tf_op jit(solution)/shard_map/ppermute | solution.py:32
  23.6 3.2 %collective-permute-start.7 = (bf16[64,3584]{1,0:T(8,128)(2,1)S(1)}, bf16[64,3584]{1,0:T(8,128)(2,1)}, u32[]{:S(2)}, u32[]{:S(2)}) collective-permute-start(bf16[64,3584]{1,0:T(8,128)(2,1)S(1)} %collective-permute-done.1.refs_1_), channel_id=1, source_target_pairs={{0,112},{8,120},{16,0},{24,8},{32,16},{40,24},{48,32},{56,40},{64,... | collective-permute-start | bytes 1376264 | tf_op jit(solution)/shard_map/ppermute | solution.py:23
  26.9 8.3 %collective-permute-done.6.refs_5_ = bf16[64,3584]{1,0:T(8,128)(2,1)} collective-permute-done((bf16[64,3584]{1,0:T(8,128)(2,1)S(1)}, bf16[64,3584]{1,0:T(8,128)(2,1)}, u32[]{:S(2)}, u32[]{:S(2)}) %collective-permute-start.6) | collective-permute-done | bytes 458784 | tf_op jit(solution)/shard_map/ppermute | solution.py:23
  36.0 3.0 %collective-permute-start.11 = (bf16[64,3584]{1,0:T(8,128)(2,1)}, bf16[64,3584]{1,0:T(8,128)(2,1)}, u32[]{:S(2)}, u32[]{:S(2)}) collective-permute-start(bf16[64,3584]{1,0:T(8,128)(2,1)} %collective-permute-done.7.refs_2_), channel_id=1, source_target_pairs={{0,8},{8,0},{16,24},{24,16},{32,40},{40,32},{48,56},{56,48},{64,72... | collective-permute-start | bytes 1376264 | tf_op jit(solution)/shard_map/ppermute | solution.py:27
  40.6 2.8 %shard_map.55 = bf16[8,128,512]{2,1,0:T(8,128)(2,1)} custom-call(s32[2]{0:T(128)S(1)} %pad_add_fusion.1.place_ref, bf16[2048,128]{1,0:T(8,128)(2,1)S(1)} %constant_dynamic-update-slice_fusion.refs_0_, bf16[2048,128]{1,0:T(8,128)(2,1)S(1)} %collective-permute-done.8.refs_1_, bf16[2048,128]{1,0:T(8,128)(2,1)S(1)} %collective-permute-done.12.refs_2_, ...), custom_call_target="tpu_custom_call" | custom-call | flops 1 | bytes 1 | tf_op jit(solution)/shard_map/pallas_call | solution.py:110
  43.4 6.4 %collective-permute-done.9.refs_6_ = bf16[64,3584]{1,0:T(8,128)(2,1)} collective-permute-done((bf16[64,3584]{1,0:T(8,128)(2,1)}, bf16[64,3584]{1,0:T(8,128)(2,1)}, u32[]{:S(2)}, u32[]{:S(2)}) %collective-permute-start.9) | collective-permute-done | bytes 458784 | tf_op jit(solution)/shard_map/ppermute | solution.py:23
  51.4 5.8 %all-to-all-start = ((bf16[8,128,512]{2,1,0:T(8,128)(2,1)}), bf16[8,128,512]{2,1,0:T(8,128)(2,1)}, u32[]{:S(2)}, u32[]{:S(2)}) async-start(bf16[8,128,512]{2,1,0:T(8,128)(2,1)} %shard_map.55), calls=%async_computation | async-start | bytes 2097152 | tf_op jit(solution)/shard_map/all_to_all | solution.py:40
  57.1 2.0 %collective-permute-start.14 = (bf16[64,3584]{1,0:T(8,128)(2,1)}, bf16[64,3584]{1,0:T(8,128)(2,1)}, u32[]{:S(2)}, u32[]{:S(2)}) collective-permute-start(bf16[64,3584]{1,0:T(8,128)(2,1)} %collective-permute-done.9.refs_6_), channel_id=1, source_target_pairs={{0,16},{8,24},{16,32},{24,40},{32,48},{40,56},{48,64},{56,72},{64,... | collective-permute-start | bytes 1376264 | tf_op jit(solution)/shard_map/ppermute | solution.py:23
  65.7 7.0 %shard_map.56 = (f32[256,896]{1,0:T(8,128)S(1)}, f32[256,896]{1,0:T(8,128)S(1)}) custom-call(s32[1]{0:T(128)} %bitcast.2.core_ref, bf16[64,3584]{1,0:T(8,128)(2,1)S(1)} %copy-done.1, bf16[64,3584]{1,0:T(8,128)(2,1)S(1)} %copy-done.5, bf16[64,3584]{1,0:T(8,128)(2,1)} %collective-permute-done.7.refs_2_, bf16[64,3584]{1,0:T(8,128)(2,1)} %collective-permute-done.10.refs_3_, ...), custom_call_target="tpu_custom_call" | custom-call | flops 1 | bytes 1 | tf_op jit(solution)/shard_map/pallas_call | solution.py:73
  73.6 18.2 %collective-permute-done.14.refs_0_ = bf16[64,3584]{1,0:T(8,128)(2,1)} collective-permute-done((bf16[64,3584]{1,0:T(8,128)(2,1)}, bf16[64,3584]{1,0:T(8,128)(2,1)}, u32[]{:S(2)}, u32[]{:S(2)}) %collective-permute-start.14) | collective-permute-done | bytes 458784 | tf_op jit(solution)/shard_map/ppermute | solution.py:23
  91.9 1.9 %collective-permute-start.20 = (bf16[64,3584]{1,0:T(8,128)(2,1)S(1)}, bf16[64,3584]{1,0:T(8,128)(2,1)S(1)}, u32[]{:S(2)}, u32[]{:S(2)}) collective-permute-start(bf16[64,3584]{1,0:T(8,128)(2,1)S(1)} %copy-done.3), channel_id=1, source_target_pairs={{0,8},{8,0},{16,24},{24,16},{32,40},{40,32},{48,56},{56,48},{64,72... | collective-permute-start | bytes 1376264 | tf_op jit(solution)/shard_map/ppermute | solution.py:27
  93.9 3.1 %collective-permute-start.19 = (bf16[64,3584]{1,0:T(8,128)(2,1)}, bf16[64,3584]{1,0:T(8,128)(2,1)S(1)}, u32[]{:S(2)}, u32[]{:S(2)}) collective-permute-start(bf16[64,3584]{1,0:T(8,128)(2,1)} %collective-permute-done.15.refs_5_), channel_id=1, source_target_pairs={{0,112},{8,120},{16,0},{24,8},{32,16},{40,24},{48,32},{56,40},{64,... | collective-permute-start | bytes 1376264 | tf_op jit(solution)/shard_map/ppermute | solution.py:23
  99.7 5.2 %collective-permute-done.20.refs_4_ = bf16[64,3584]{1,0:T(8,128)(2,1)S(1)} collective-permute-done((bf16[64,3584]{1,0:T(8,128)(2,1)S(1)}, bf16[64,3584]{1,0:T(8,128)(2,1)S(1)}, u32[]{:S(2)}, u32[]{:S(2)}) %collective-permute-start.20) | collective-permute-done | bytes 458784 | tf_op jit(solution)/shard_map/ppermute | solution.py:27
  108.0 6.7 %all-to-all-start.1 = ((bf16[16,128,512]{2,1,0:T(8,128)(2,1)}), bf16[16,128,512]{2,1,0:T(8,128)(2,1)S(1)}, u32[]{:S(2)}, u32[]{:S(2)}) async-start(bf16[16,128,512]{2,1,0:T(8,128)(2,1)} %broadcast_in_dim.21), calls=%async_computation.1 | async-start | bytes 4194304 | tf_op jit(solution)/shard_map/all_to_all | solution.py:268
  116.8 7.0 %shard_map.59 = (f32[256,896]{1,0:T(8,128)S(1)}, f32[256,896]{1,0:T(8,128)S(1)}) custom-call(s32[1]{0:T(128)} %bitcast.2.core_ref, bf16[64,3584]{1,0:T(8,128)(2,1)} %collective-permute-done.14.refs_0_, bf16[64,3584]{1,0:T(8,128)(2,1)} %collective-permute-done.17.refs_1_, bf16[64,3584]{1,0:T(8,128)(2,1)} %collective-permute-done.21.refs_2_, ...), custom_call_target="tpu_custom_call" | custom-call | flops 1 | bytes 1 | tf_op jit(solution)/shard_map/pallas_call | solution.py:73
  126.1 1.9 %collective-permute-start.24 = (f32[64,896]{1,0:T(8,128)S(1)}, f32[64,896]{1,0:T(8,128)S(1)}, u32[]{:S(2)}, u32[]{:S(2)}) collective-permute-start(f32[64,896]{1,0:T(8,128)S(1)} %get-tuple-element.86), channel_id=1, source_target_pairs={{0,4},{1,5},{2,6},{3,7},{4,0},{5,1},{6,2},{7,3},{8,12},{9,13},{10,... | collective-permute-start | bytes 688136 | tf_op jit(solution)/shard_map/ppermute | solution.py:32
  130.2 2.9 %collective-permute-start.32 = (f32[64,896]{1,0:T(8,128)S(1)}, f32[64,896]{1,0:T(8,128)S(1)}, u32[]{:S(2)}, u32[]{:S(2)}) collective-permute-start(f32[64,896]{1,0:T(8,128)S(1)} %get-tuple-element.99), channel_id=1, source_target_pairs={{0,4},{1,5},{2,6},{3,7},{4,0},{5,1},{6,2},{7,3},{8,12},{9,13},{10,... | collective-permute-start | bytes 688136 | tf_op jit(solution)/shard_map/ppermute | solution.py:32
  133.1 3.5 %collective-permute-done.23 = f32[64,896]{1,0:T(8,128)S(1)} collective-permute-done((f32[64,896]{1,0:T(8,128)S(1)}, f32[64,896]{1,0:T(8,128)S(1)}, u32[]{:S(2)}, u32[]{:S(2)}) %collective-permute-start.23) | collective-permute-done | bytes 229408 | tf_op jit(solution)/shard_map/ppermute | solution.py:32
  136.6 3.0 %collective-permute-start.33 = (f32[64,896]{1,0:T(8,128)S(1)}, f32[64,896]{1,0:T(8,128)S(1)}, u32[]{:S(2)}, u32[]{:S(2)}) collective-permute-start(f32[64,896]{1,0:T(8,128)S(1)} %get-tuple-element.100), channel_id=1, source_target_pairs={{0,6},{1,7},{2,0},{3,1},{4,2},{5,3},{6,4},{7,5},{8,14},{9,15},{10,... | collective-permute-start | bytes 688136 | tf_op jit(solution)/shard_map/ppermute | solution.py:32
  141.8 1.9 %collective-permute-start.27 = (bf16[64,896]{1,0:T(8,128)(2,1)S(1)}, bf16[64,896]{1,0:T(8,128)(2,1)S(1)}, u32[]{:S(2)}, u32[]{:S(2)}) collective-permute-start(bf16[64,896]{1,0:T(8,128)(2,1)S(1)} %add_convert_fusion.1.refs_0_), channel_id=1, source_target_pairs={{0,4},{1,5},{2,6},{3,7},{4,0},{5,1},{6,2},{7,3},{8,12},{9,13},{10,... | collective-permute-start | bytes 344072 | tf_op jit(solution)/shard_map/ppermute | solution.py:32
  143.7 2.1 %collective-permute-start.26 = (bf16[64,896]{1,0:T(8,128)(2,1)S(1)}, bf16[64,896]{1,0:T(8,128)(2,1)S(1)}, u32[]{:S(2)}, u32[]{:S(2)}) collective-permute-start(bf16[64,896]{1,0:T(8,128)(2,1)S(1)} %add_convert_fusion.1.refs_0_), channel_id=1, source_target_pairs={{0,6},{1,7},{2,0},{3,1},{4,2},{5,3},{6,4},{7,5},{8,14},{9,15},{10,... | collective-permute-start | bytes 344072 | tf_op jit(solution)/shard_map/ppermute | solution.py:32
  146.1 4.9 %collective-permute-done.33 = f32[64,896]{1,0:T(8,128)S(1)} collective-permute-done((f32[64,896]{1,0:T(8,128)S(1)}, f32[64,896]{1,0:T(8,128)S(1)}, u32[]{:S(2)}, u32[]{:S(2)}) %collective-permute-start.33) | collective-permute-done | bytes 229408 | tf_op jit(solution)/shard_map/ppermute | solution.py:32
  151.7 1.9 %collective-permute-start.35 = (bf16[64,896]{1,0:T(8,128)(2,1)S(1)}, bf16[64,896]{1,0:T(8,128)(2,1)S(1)}, u32[]{:S(2)}, u32[]{:S(2)}) collective-permute-start(bf16[64,896]{1,0:T(8,128)(2,1)S(1)} %add_convert_fusion.refs_0_), channel_id=1, source_target_pairs={{0,4},{1,5},{2,6},{3,7},{4,0},{5,1},{6,2},{7,3},{8,12},{9,13},{10,... | collective-permute-start | bytes 344072 | tf_op jit(solution)/shard_map/ppermute | solution.py:32
  153.5 2.3 %collective-permute-start.34 = (bf16[64,896]{1,0:T(8,128)(2,1)S(1)}, bf16[64,896]{1,0:T(8,128)(2,1)S(1)}, u32[]{:S(2)}, u32[]{:S(2)}) collective-permute-start(bf16[64,896]{1,0:T(8,128)(2,1)S(1)} %add_convert_fusion.refs_0_), channel_id=1, source_target_pairs={{0,6},{1,7},{2,0},{3,1},{4,2},{5,3},{6,4},{7,5},{8,14},{9,15},{10,... | collective-permute-start | bytes 344072 | tf_op jit(solution)/shard_map/ppermute | solution.py:32
  156.4 2.4 %collective-permute-done.35.refs_2_ = bf16[64,896]{1,0:T(8,128)(2,1)S(1)} collective-permute-done((bf16[64,896]{1,0:T(8,128)(2,1)S(1)}, bf16[64,896]{1,0:T(8,128)(2,1)S(1)}, u32[]{:S(2)}, u32[]{:S(2)}) %collective-permute-start.35) | collective-permute-done | bytes 114720 | tf_op jit(solution)/shard_map/ppermute | solution.py:32
  161.9 3.4 %all-to-all-done.1 = bf16[16,128,512]{2,1,0:T(8,128)(2,1)S(1)} async-done(((bf16[16,128,512]{2,1,0:T(8,128)(2,1)}), bf16[16,128,512]{2,1,0:T(8,128)(2,1)S(1)}, u32[]{:S(2)}, u32[]{:S(2)}) %all-to-all-start.1) | async-done | bytes 2097184 | tf_op jit(solution)/shard_map/all_to_all | solution.py:268
  165.3 6.7 %shard_map.62 = f32[1024,896]{1,0:T(8,128)} custom-call(s32[3]{0:T(128)S(1)} %pad_add_fusion.place_ref, f32[1]{0:T(128)} %bitcast.4.scale_ref, bf16[8,2,128,512]{3,2,1,0:T(8,128)(2,1)S(1)} %bitcast.7, bf16[256,896]{1,0:T(8,128)(2,1)S(1)} %shard_map.58.refs_1_, bf16[256,896]{1,0:T(8,128)(2,1)S(1)} %collective-permute-done.29.refs_2_, ...), custom_call_target="tpu_custom_call" | custom-call | flops 1 | bytes 1 | tf_op jit(solution)/shard_map/pallas_call | solution.py:199
  (97 shorter events, 35.0 us)
Async XLA Ops:
  1.3 21.6 %collective-permute-start.2 = (bf16[512,512]{1,0:T(8,128)(2,1)S(1)}, bf16[512,512]{1,0:T(8,128)(2,1)S(1)}, u32[]{:S(2)}, u32[]{:S(2)}) collective-permute-start(bf16[512,512]{1,0:T(8,128)(2,1)S(1)} %get-tuple-element.101), channel_id=1, source_target_pairs={{0,8},{8,0},{16,24},{24,16},{32,40},{40,32},{48,56},{56,48},{64,72... | collective-permute-start | bytes 1572872 | tf_op jit(solution)/shard_map/ppermute | solution.py:27
  4.5 18.5 %collective-permute-start = (bf16[64,3584]{1,0:T(8,128)(2,1)S(1)}, bf16[64,3584]{1,0:T(8,128)(2,1)S(1)}, u32[]{:S(2)}, u32[]{:S(2)}) collective-permute-start(bf16[64,3584]{1,0:T(8,128)(2,1)S(1)} %copy-done), channel_id=1, source_target_pairs={{0,16},{8,24},{16,32},{24,40},{32,48},{40,56},{48,64},{56,72},{64,... | collective-permute-start | bytes 1376264 | tf_op jit(solution)/shard_map/ppermute | solution.py:23
  6.4 16.5 %collective-permute-start.1 = (bf16[64,3584]{1,0:T(8,128)(2,1)S(1)}, bf16[64,3584]{1,0:T(8,128)(2,1)S(1)}, u32[]{:S(2)}, u32[]{:S(2)}) collective-permute-start(bf16[64,3584]{1,0:T(8,128)(2,1)S(1)} %copy-done), channel_id=1, source_target_pairs={{0,112},{8,120},{16,0},{24,8},{32,16},{40,24},{48,32},{56,40},{64,... | collective-permute-start | bytes 1376264 | tf_op jit(solution)/shard_map/ppermute | solution.py:23
  10.3 7.6 %collective-permute-start.4 = (bf16[512,128]{1,0:T(8,128)(2,1)S(1)}, bf16[512,128]{1,0:T(8,128)(2,1)S(1)}, u32[]{:S(2)}, u32[]{:S(2)}) collective-permute-start(bf16[512,128]{1,0:T(8,128)(2,1)S(1)} %copy-done.11), channel_id=1, source_target_pairs={{0,4},{1,5},{2,6},{3,7},{4,0},{5,1},{6,2},{7,3},{8,12},{9,13},{10,... | collective-permute-start | bytes 393224 | tf_op jit(solution)/shard_map/ppermute | solution.py:32
  12.6 6.7 %collective-permute-start.3 = (bf16[512,128]{1,0:T(8,128)(2,1)S(1)}, bf16[512,128]{1,0:T(8,128)(2,1)S(1)}, u32[]{:S(2)}, u32[]{:S(2)}) collective-permute-start(bf16[512,128]{1,0:T(8,128)(2,1)S(1)} %copy-done.11), channel_id=1, source_target_pairs={{0,6},{1,7},{2,0},{3,1},{4,2},{5,3},{6,4},{7,5},{8,14},{9,15},{10,... | collective-permute-start | bytes 393224 | tf_op jit(solution)/shard_map/ppermute | solution.py:32
  23.0 12.1 %collective-permute-start.8 = (bf16[2048,128]{1,0:T(8,128)(2,1)S(1)}, bf16[2048,128]{1,0:T(8,128)(2,1)S(1)}, u32[]{:S(2)}, u32[]{:S(2)}) collective-permute-start(bf16[2048,128]{1,0:T(8,128)(2,1)S(1)} %constant_dynamic-update-slice_fusion.refs_0_), channel_id=1, source_target_pairs={{0,8},{8,0},{16,24},{24,16},{32,40},{40,32},{48,56},{56,48},{64,72... | collective-permute-start | bytes 1572872 | tf_op jit(solution)/shard_map/ppermute | solution.py:27
  23.6 11.5 %collective-permute-start.6 = (bf16[64,3584]{1,0:T(8,128)(2,1)S(1)}, bf16[64,3584]{1,0:T(8,128)(2,1)}, u32[]{:S(2)}, u32[]{:S(2)}) collective-permute-start(bf16[64,3584]{1,0:T(8,128)(2,1)S(1)} %collective-permute-done.refs_4_), channel_id=1, source_target_pairs={{0,16},{8,24},{16,32},{24,40},{32,48},{40,56},{48,64},{56,72},{64,... | collective-permute-start | bytes 1376264 | tf_op jit(solution)/shard_map/ppermute | solution.py:23
  23.6 11.5 %collective-permute-start.7 = (bf16[64,3584]{1,0:T(8,128)(2,1)S(1)}, bf16[64,3584]{1,0:T(8,128)(2,1)}, u32[]{:S(2)}, u32[]{:S(2)}) collective-permute-start(bf16[64,3584]{1,0:T(8,128)(2,1)S(1)} %collective-permute-done.1.refs_1_), channel_id=1, source_target_pairs={{0,112},{8,120},{16,0},{24,8},{32,16},{40,24},{48,32},{56,40},{64,... | collective-permute-start | bytes 1376264 | tf_op jit(solution)/shard_map/ppermute | solution.py:23
  35.7 14.1 %collective-permute-start.9 = (bf16[64,3584]{1,0:T(8,128)(2,1)}, bf16[64,3584]{1,0:T(8,128)(2,1)}, u32[]{:S(2)}, u32[]{:S(2)}) collective-permute-start(bf16[64,3584]{1,0:T(8,128)(2,1)} %collective-permute-done.6.refs_5_), channel_id=1, source_target_pairs={{0,16},{8,24},{16,32},{24,40},{32,48},{40,56},{48,64},{56,72},{64,... | collective-permute-start | bytes 1376264 | tf_op jit(solution)/shard_map/ppermute | solution.py:23
  36.0 14.1 %collective-permute-start.11 = (bf16[64,3584]{1,0:T(8,128)(2,1)}, bf16[64,3584]{1,0:T(8,128)(2,1)}, u32[]{:S(2)}, u32[]{:S(2)}) collective-permute-start(bf16[64,3584]{1,0:T(8,128)(2,1)} %collective-permute-done.7.refs_2_), channel_id=1, source_target_pairs={{0,8},{8,0},{16,24},{24,16},{32,40},{40,32},{48,56},{56,48},{64,72... | collective-permute-start | bytes 1376264 | tf_op jit(solution)/shard_map/ppermute | solution.py:27
  39.1 12.3 %collective-permute-start.10 = (bf16[64,3584]{1,0:T(8,128)(2,1)}, bf16[64,3584]{1,0:T(8,128)(2,1)}, u32[]{:S(2)}, u32[]{:S(2)}) collective-permute-start(bf16[64,3584]{1,0:T(8,128)(2,1)} %collective-permute-done.7.refs_2_), channel_id=1, source_target_pairs={{0,112},{8,120},{16,0},{24,8},{32,16},{40,24},{48,32},{56,40},{64,... | collective-permute-start | bytes 1376264 | tf_op jit(solution)/shard_map/ppermute | solution.py:23
  51.4 46.9 %all-to-all-start = ((bf16[8,128,512]{2,1,0:T(8,128)(2,1)}), bf16[8,128,512]{2,1,0:T(8,128)(2,1)}, u32[]{:S(2)}, u32[]{:S(2)}) async-start(bf16[8,128,512]{2,1,0:T(8,128)(2,1)} %shard_map.55), calls=%async_computation | async-start | bytes 2097152 | tf_op jit(solution)/shard_map/all_to_all | solution.py:40
  57.1 34.7 %collective-permute-start.14 = (bf16[64,3584]{1,0:T(8,128)(2,1)}, bf16[64,3584]{1,0:T(8,128)(2,1)}, u32[]{:S(2)}, u32[]{:S(2)}) collective-permute-start(bf16[64,3584]{1,0:T(8,128)(2,1)} %collective-permute-done.9.refs_6_), channel_id=1, source_target_pairs={{0,16},{8,24},{16,32},{24,40},{32,48},{40,56},{48,64},{56,72},{64,... | collective-permute-start | bytes 1376264 | tf_op jit(solution)/shard_map/ppermute | solution.py:23
  59.1 32.7 %collective-permute-start.15 = (bf16[64,3584]{1,0:T(8,128)(2,1)}, bf16[64,3584]{1,0:T(8,128)(2,1)}, u32[]{:S(2)}, u32[]{:S(2)}) collective-permute-start(bf16[64,3584]{1,0:T(8,128)(2,1)} %collective-permute-done.11.refs_7_), channel_id=1, source_target_pairs={{0,112},{8,120},{16,0},{24,8},{32,16},{40,24},{48,32},{56,40},{64,... | collective-permute-start | bytes 1376264 | tf_op jit(solution)/shard_map/ppermute | solution.py:23
  60.4 31.5 %collective-permute-start.16 = (bf16[64,3584]{1,0:T(8,128)(2,1)}, bf16[64,3584]{1,0:T(8,128)(2,1)}, u32[]{:S(2)}, u32[]{:S(2)}) collective-permute-start(bf16[64,3584]{1,0:T(8,128)(2,1)} %collective-permute-done.6.refs_5_), channel_id=1, source_target_pairs={{0,8},{8,0},{16,24},{24,16},{32,40},{40,32},{48,56},{56,48},{64,72... | collective-permute-start | bytes 1376264 | tf_op jit(solution)/shard_map/ppermute | solution.py:27
  62.2 29.7 %collective-permute-start.17 = (bf16[64,3584]{1,0:T(8,128)(2,1)}, bf16[64,3584]{1,0:T(8,128)(2,1)}, u32[]{:S(2)}, u32[]{:S(2)}) collective-permute-start(bf16[64,3584]{1,0:T(8,128)(2,1)} %copy-done.4), channel_id=1, source_target_pairs={{0,8},{8,0},{16,24},{24,16},{32,40},{40,32},{48,56},{56,48},{64,72... | collective-permute-start | bytes 1376264 | tf_op jit(solution)/shard_map/ppermute | solution.py:27
  63.9 35.8 %collective-permute-start.21 = (bf16[64,3584]{1,0:T(8,128)(2,1)S(1)}, bf16[64,3584]{1,0:T(8,128)(2,1)}, u32[]{:S(2)}, u32[]{:S(2)}) collective-permute-start(bf16[64,3584]{1,0:T(8,128)(2,1)S(1)} %copy-done.1), channel_id=1, source_target_pairs={{0,8},{8,0},{16,24},{24,16},{32,40},{40,32},{48,56},{56,48},{64,72... | collective-permute-start | bytes 1376264 | tf_op jit(solution)/shard_map/ppermute | solution.py:27
  91.9 13.1 %collective-permute-start.20 = (bf16[64,3584]{1,0:T(8,128)(2,1)S(1)}, bf16[64,3584]{1,0:T(8,128)(2,1)S(1)}, u32[]{:S(2)}, u32[]{:S(2)}) collective-permute-start(bf16[64,3584]{1,0:T(8,128)(2,1)S(1)} %copy-done.3), channel_id=1, source_target_pairs={{0,8},{8,0},{16,24},{24,16},{32,40},{40,32},{48,56},{56,48},{64,72... | collective-permute-start | bytes 1376264 | tf_op jit(solution)/shard_map/ppermute | solution.py:27
  93.8 12.6 %collective-permute-start.18 = (bf16[64,3584]{1,0:T(8,128)(2,1)}, bf16[64,3584]{1,0:T(8,128)(2,1)S(1)}, u32[]{:S(2)}, u32[]{:S(2)}) collective-permute-start(bf16[64,3584]{1,0:T(8,128)(2,1)} %collective-permute-done.16.refs_3_), channel_id=1, source_target_pairs={{0,16},{8,24},{16,32},{24,40},{32,48},{40,56},{48,64},{56,72},{64,... | collective-permute-start | bytes 1376264 | tf_op jit(solution)/shard_map/ppermute | solution.py:23
  93.9 12.5 %collective-permute-start.19 = (bf16[64,3584]{1,0:T(8,128)(2,1)}, bf16[64,3584]{1,0:T(8,128)(2,1)S(1)}, u32[]{:S(2)}, u32[]{:S(2)}) collective-permute-start(bf16[64,3584]{1,0:T(8,128)(2,1)} %collective-permute-done.15.refs_5_), channel_id=1, source_target_pairs={{0,112},{8,120},{16,0},{24,8},{32,16},{40,24},{48,32},{56,40},{64,... | collective-permute-start | bytes 1376264 | tf_op jit(solution)/shard_map/ppermute | solution.py:23
  108.0 57.3 %all-to-all-start.1 = ((bf16[16,128,512]{2,1,0:T(8,128)(2,1)}), bf16[16,128,512]{2,1,0:T(8,128)(2,1)S(1)}, u32[]{:S(2)}, u32[]{:S(2)}) async-start(bf16[16,128,512]{2,1,0:T(8,128)(2,1)} %broadcast_in_dim.21), calls=%async_computation.1 | async-start | bytes 4194304 | tf_op jit(solution)/shard_map/all_to_all | solution.py:268
  114.7 9.7 %collective-permute-start.22 = (f32[256,896]{1,0:T(8,128)}, f32[256,896]{1,0:T(8,128)S(1)}, u32[]{:S(2)}, u32[]{:S(2)}) collective-permute-start(f32[256,896]{1,0:T(8,128)} %copy-done.10), channel_id=1, source_target_pairs={{0,1},{1,0},{2,3},{3,2},{4,5},{5,4},{6,7},{7,6},{8,9},{9,8},{10,11... | collective-permute-start | bytes 2752520 | tf_op jit(solution)/shard_map/ppermute | solution.py:36
  124.5 12.1 %collective-permute-start.23 = (f32[64,896]{1,0:T(8,128)S(1)}, f32[64,896]{1,0:T(8,128)S(1)}, u32[]{:S(2)}, u32[]{:S(2)}) collective-permute-start(f32[64,896]{1,0:T(8,128)S(1)} %get-tuple-element.85), channel_id=1, source_target_pairs={{0,2},{1,3},{2,4},{3,5},{4,6},{5,7},{6,0},{7,1},{8,10},{9,11},{10,... | collective-permute-start | bytes 688136 | tf_op jit(solution)/shard_map/ppermute | solution.py:32
  126.1 13.4 %collective-permute-start.24 = (f32[64,896]{1,0:T(8,128)S(1)}, f32[64,896]{1,0:T(8,128)S(1)}, u32[]{:S(2)}, u32[]{:S(2)}) collective-permute-start(f32[64,896]{1,0:T(8,128)S(1)} %get-tuple-element.86), channel_id=1, source_target_pairs={{0,4},{1,5},{2,6},{3,7},{4,0},{5,1},{6,2},{7,3},{8,12},{9,13},{10,... | collective-permute-start | bytes 688136 | tf_op jit(solution)/shard_map/ppermute | solution.py:32
  128.0 13.1 %collective-permute-start.25 = (f32[64,896]{1,0:T(8,128)S(1)}, f32[64,896]{1,0:T(8,128)S(1)}, u32[]{:S(2)}, u32[]{:S(2)}) collective-permute-start(f32[64,896]{1,0:T(8,128)S(1)} %get-tuple-element.87), channel_id=1, source_target_pairs={{0,6},{1,7},{2,0},{3,1},{4,2},{5,3},{6,4},{7,5},{8,14},{9,15},{10,... | collective-permute-start | bytes 688136 | tf_op jit(solution)/shard_map/ppermute | solution.py:32
  129.6 14.1 %collective-permute-start.31 = (f32[64,896]{1,0:T(8,128)S(1)}, f32[64,896]{1,0:T(8,128)S(1)}, u32[]{:S(2)}, u32[]{:S(2)}) collective-permute-start(f32[64,896]{1,0:T(8,128)S(1)} %get-tuple-element.98), channel_id=1, source_target_pairs={{0,2},{1,3},{2,4},{3,5},{4,6},{5,7},{6,0},{7,1},{8,10},{9,11},{10,... | collective-permute-start | bytes 688136 | tf_op jit(solution)/shard_map/ppermute | solution.py:32
  130.2 15.8 %collective-permute-start.32 = (f32[64,896]{1,0:T(8,128)S(1)}, f32[64,896]{1,0:T(8,128)S(1)}, u32[]{:S(2)}, u32[]{:S(2)}) collective-permute-start(f32[64,896]{1,0:T(8,128)S(1)} %get-tuple-element.99), channel_id=1, source_target_pairs={{0,4},{1,5},{2,6},{3,7},{4,0},{5,1},{6,2},{7,3},{8,12},{9,13},{10,... | collective-permute-start | bytes 688136 | tf_op jit(solution)/shard_map/ppermute | solution.py:32
  136.6 14.4 %collective-permute-start.33 = (f32[64,896]{1,0:T(8,128)S(1)}, f32[64,896]{1,0:T(8,128)S(1)}, u32[]{:S(2)}, u32[]{:S(2)}) collective-permute-start(f32[64,896]{1,0:T(8,128)S(1)} %get-tuple-element.100), channel_id=1, source_target_pairs={{0,6},{1,7},{2,0},{3,1},{4,2},{5,3},{6,4},{7,5},{8,14},{9,15},{10,... | collective-permute-start | bytes 688136 | tf_op jit(solution)/shard_map/ppermute | solution.py:32
  141.2 12.3 %collective-permute-start.28 = (bf16[64,896]{1,0:T(8,128)(2,1)S(1)}, bf16[64,896]{1,0:T(8,128)(2,1)S(1)}, u32[]{:S(2)}, u32[]{:S(2)}) collective-permute-start(bf16[64,896]{1,0:T(8,128)(2,1)S(1)} %add_convert_fusion.1.refs_0_), channel_id=1, source_target_pairs={{0,2},{1,3},{2,4},{3,5},{4,6},{5,7},{6,0},{7,1},{8,10},{9,11},{10,... | collective-permute-start | bytes 344072 | tf_op jit(solution)/shard_map/ppermute | solution.py:32
  141.8 14.0 %collective-permute-start.27 = (bf16[64,896]{1,0:T(8,128)(2,1)S(1)}, bf16[64,896]{1,0:T(8,128)(2,1)S(1)}, u32[]{:S(2)}, u32[]{:S(2)}) collective-permute-start(bf16[64,896]{1,0:T(8,128)(2,1)S(1)} %add_convert_fusion.1.refs_0_), channel_id=1, source_target_pairs={{0,4},{1,5},{2,6},{3,7},{4,0},{5,1},{6,2},{7,3},{8,12},{9,13},{10,... | collective-permute-start | bytes 344072 | tf_op jit(solution)/shard_map/ppermute | solution.py:32
  143.7 12.2 %collective-permute-start.26 = (bf16[64,896]{1,0:T(8,128)(2,1)S(1)}, bf16[64,896]{1,0:T(8,128)(2,1)S(1)}, u32[]{:S(2)}, u32[]{:S(2)}) collective-permute-start(bf16[64,896]{1,0:T(8,128)(2,1)S(1)} %add_convert_fusion.1.refs_0_), channel_id=1, source_target_pairs={{0,6},{1,7},{2,0},{3,1},{4,2},{5,3},{6,4},{7,5},{8,14},{9,15},{10,... | collective-permute-start | bytes 344072 | tf_op jit(solution)/shard_map/ppermute | solution.py:32
  151.7 7.2 %collective-permute-start.35 = (bf16[64,896]{1,0:T(8,128)(2,1)S(1)}, bf16[64,896]{1,0:T(8,128)(2,1)S(1)}, u32[]{:S(2)}, u32[]{:S(2)}) collective-permute-start(bf16[64,896]{1,0:T(8,128)(2,1)S(1)} %add_convert_fusion.refs_0_), channel_id=1, source_target_pairs={{0,4},{1,5},{2,6},{3,7},{4,0},{5,1},{6,2},{7,3},{8,12},{9,13},{10,... | collective-permute-start | bytes 344072 | tf_op jit(solution)/shard_map/ppermute | solution.py:32
  (21 other events, 184.4 us)

commit v4 on v3

--- a/solution.py
+++ b/solution.py
@@ -89,14 +89,15 @@
 def partial_kernel(place_ref, *refs):
     grads, (near_ref, far_ref, out_ref) = refs[:4], refs[4:]
     y, core = place_ref[0], place_ref[1]
-    rows = near_ref.shape[0]
+    rows, cols = far_ref.shape
+    own = pl.ds(pl.multiple_of(place_ref[2] * cols, 128), cols)
     lefts = []
     for near, far in (grads[:2], grads[2:]):
         for k in range(Y):
             part = pl.ds(k * rows, rows)
             lefts.append(jnp.concatenate([near[part, :], far[part, :]], axis=0))
     left = jnp.concatenate(lefts, axis=1)
-    right = jnp.concatenate([near_ref[...], far_ref[...]], axis=0)
+    right = jnp.concatenate([near_ref[:, own], far_ref[...]], axis=0)
     term = lax.dot_general(left, right, (((0,), (0,)), ((), ())), preferred_element_type=jnp.float32)
     for n in range(SEQS):
         owner = jnp.where(n < Y, core, 1 - core)
@@ -105,7 +106,7 @@
 
 
 def partial_out(grads, near, far, place):
-    cols = near.shape[1]
+    cols = far.shape[1]
     vmem = pl.BlockSpec(memory_space=pltpu.VMEM)
     return pl.pallas_call(
         partial_kernel,
@@ -231,9 +232,8 @@
     a[0] = activations
     a[-1], a[1] = shift_z(a[0], 1), shift_z(a[0], -1)
     far = swap_x(lax.dynamic_slice(basis_out, (0, (1 - h) * half_cols), (rows, half_cols)))
-    near = lax.dynamic_slice(basis_out, (0, h * half_cols), (rows, half_cols))
     grads = [grads_out] + [shift_y(grads_out, -k) for k in (1, 2, 3)]
-    a[-1], a[1], near, far, *grads = together(a[-1], a[1], near, far, *grads)
+    a[-1], a[1], far, *grads = together(a[-1], a[1], far, *grads)
 
     a[-2], a[2] = shift_z(a[-1], 1), shift_z(a[1], -1)
     grads_near = jnp.concatenate(grads, axis=0)
@@ -242,7 +242,7 @@
 
     a[-3], a[3], c[2] = shift_z(a[-2], 1), shift_z(a[2], -1), swap_x(a[2])
     grads = [grads_near, grads_far, swap_core(grads_near), swap_core(grads_far)]
-    part = partial_out(grads, near, far, jnp.stack([y, core]))
+    part = partial_out(grads, basis_out, far, jnp.stack([y, core, h]))
     a[-3], a[3], c[2], part, a[1], a[-2], a[-1], a[0], basis_in = together(
         a[-3], a[3], c[2], part, a[1], a[-2], a[-1], a[0], basis_in
     )

time: 172 us -> 174 us (1.012)
    unnamed x29 -> x27, local copies, waits for them, and re-layouts: 3.05 us -> 4.12 us
where the time goes in v4:
time: 174 us; the launch traced here: 173 us
  starting transfers between devices  70.9 us (41%)
  waiting for transfers between devices  66.8 us (38%)
  Pallas kernels  24.3 us (14%)
  local copies, waits for them, and re-layouts  7.49 us (4%)
  other arithmetic  2.97 us (2%)
    ppermute x10, waiting for transfers between devices, shift_z(): return lax.ppermute(x, 'wide', pairs)  34.2 us
    ppermute x15, starting transfers between devices, shift_y(): return lax.ppermute(x, 'tp', pairs)  25.8 us
    ppermute x15, waiting for transfers between devices, shift_y(): return lax.ppermute(x, 'tp', pairs)  21.9 us
    ppermute x10, starting transfers between devices, shift_z(): return lax.ppermute(x, 'wide', pairs)  17.6 us
    pallas_call x2, Pallas kernels, rotate_in(): pl.pallas_call(functools.partial(rotate_kernel, count), out_shape=(shape,...  14 us
    ppermute x7, starting transfers between devices, swap_x(): return lax.ppermute(x, 'wide', [(i, i ^ 1) for i in range(2 * Z)])  13.3 us
    all_to_all x1, starting transfers between devices, on_device(): rotated_out = lax.all_to_all(copies, 'wide', 0, 0, tiled=True)  7.08 us
    pallas_call x1, Pallas kernels, products(): pl.pallas_call(functools.partial(products_kernel, layout), out_shape=jax....  6.73 us
  transfers between devices with their start and end apart: 40, of which 19 were waited for; matrix products, arithmetic and copies ran while one was open for 2% of the time, Pallas kernels for 10%

profile of v4, /device:TPU:8, one launch (start us, length us, event | category | flops | bytes accessed | tf_op | source)
XLA Modules:
  0.0 173.4 jit_solution(2812504571130564617)
XLA Ops:
  1.2 3.1 %collective-permute-start.2 = (bf16[512,512]{1,0:T(8,128)(2,1)S(1)}, bf16[512,512]{1,0:T(8,128)(2,1)S(1)}, u32[]{:S(2)}, u32[]{:S(2)}) collective-permute-start(bf16[512,512]{1,0:T(8,128)(2,1)S(1)} %constant_dynamic-slice_fusion), channel_id=1, source_target_pairs={{0,8},{8,0},{16,24},{24,16},{32,40},{40,32},{48,56},{56,48},{64,72... | collective-permute-start | bytes 1572872 | tf_op jit(solution)/shard_map/ppermute | solution.py:27
  4.3 1.9 %collective-permute-start = (bf16[64,3584]{1,0:T(8,128)(2,1)}, bf16[64,3584]{1,0:T(8,128)(2,1)S(1)}, u32[]{:S(2)}, u32[]{:S(2)}) collective-permute-start(bf16[64,3584]{1,0:T(8,128)(2,1)} %refs_0_), channel_id=1, source_target_pairs={{0,16},{8,24},{16,32},{24,40},{32,48},{40,56},{48,64},{56,72},{64,... | collective-permute-start | bytes 1376264 | tf_op jit(solution)/shard_map/ppermute | solution.py:23
  6.2 3.9 %collective-permute-start.1 = (bf16[64,3584]{1,0:T(8,128)(2,1)}, bf16[64,3584]{1,0:T(8,128)(2,1)S(1)}, u32[]{:S(2)}, u32[]{:S(2)}) collective-permute-start(bf16[64,3584]{1,0:T(8,128)(2,1)} %refs_0_), channel_id=1, source_target_pairs={{0,112},{8,120},{16,0},{24,8},{32,16},{40,24},{48,32},{56,40},{64,... | collective-permute-start | bytes 1376264 | tf_op jit(solution)/shard_map/ppermute | solution.py:23
  10.1 2.3 %collective-permute-start.4 = (bf16[512,128]{1,0:T(8,128)(2,1)}, bf16[512,128]{1,0:T(8,128)(2,1)S(1)}, u32[]{:S(2)}, u32[]{:S(2)}) collective-permute-start(bf16[512,128]{1,0:T(8,128)(2,1)} %param.6), channel_id=1, source_target_pairs={{0,4},{1,5},{2,6},{3,7},{4,0},{5,1},{6,2},{7,3},{8,12},{9,13},{10,... | collective-permute-start | bytes 393224 | tf_op jit(solution)/shard_map/ppermute | solution.py:32
  13.8 4.2 %collective-permute-done.4 = bf16[512,128]{1,0:T(8,128)(2,1)S(1)} collective-permute-done((bf16[512,128]{1,0:T(8,128)(2,1)}, bf16[512,128]{1,0:T(8,128)(2,1)S(1)}, u32[]{:S(2)}, u32[]{:S(2)}) %collective-permute-start.4) | collective-permute-done | bytes 131104 | tf_op jit(solution)/shard_map/ppermute | solution.py:32
  19.3 3.8 %collective-permute-done.5 = bf16[512,128]{1,0:T(8,128)(2,1)S(1)} collective-permute-done((bf16[512,128]{1,0:T(8,128)(2,1)}, bf16[512,128]{1,0:T(8,128)(2,1)S(1)}, u32[]{:S(2)}, u32[]{:S(2)}) %collective-permute-start.5) | collective-permute-done | bytes 131104 | tf_op jit(solution)/shard_map/ppermute | solution.py:32
  24.9 3.2 %collective-permute-start.7 = (bf16[64,3584]{1,0:T(8,128)(2,1)S(1)}, bf16[64,3584]{1,0:T(8,128)(2,1)}, u32[]{:S(2)}, u32[]{:S(2)}) collective-permute-start(bf16[64,3584]{1,0:T(8,128)(2,1)S(1)} %collective-permute-done.1.refs_1_), channel_id=1, source_target_pairs={{0,112},{8,120},{16,0},{24,8},{32,16},{40,24},{48,32},{56,40},{64,... | collective-permute-start | bytes 1376264 | tf_op jit(solution)/shard_map/ppermute | solution.py:23
  28.2 7.7 %collective-permute-done.6.refs_5_ = bf16[64,3584]{1,0:T(8,128)(2,1)} collective-permute-done((bf16[64,3584]{1,0:T(8,128)(2,1)S(1)}, bf16[64,3584]{1,0:T(8,128)(2,1)}, u32[]{:S(2)}, u32[]{:S(2)}) %collective-permute-start.6) | collective-permute-done | bytes 458784 | tf_op jit(solution)/shard_map/ppermute | solution.py:23
  37.1 3.0 %collective-permute-start.11 = (bf16[64,3584]{1,0:T(8,128)(2,1)}, bf16[64,3584]{1,0:T(8,128)(2,1)}, u32[]{:S(2)}, u32[]{:S(2)}) collective-permute-start(bf16[64,3584]{1,0:T(8,128)(2,1)} %collective-permute-done.7.refs_2_), channel_id=1, source_target_pairs={{0,8},{8,0},{16,24},{24,16},{32,40},{40,32},{48,56},{56,48},{64,72... | collective-permute-start | bytes 1376264 | tf_op jit(solution)/shard_map/ppermute | solution.py:27
  41.8 3.3 %shard_map.55 = bf16[8,128,512]{2,1,0:T(8,128)(2,1)} custom-call(s32[3]{0:T(128)S(1)} %pad_add_fusion.1.place_ref, bf16[2048,128]{1,0:T(8,128)(2,1)S(1)} %constant_dynamic-update-slice_fusion.refs_0_, bf16[2048,128]{1,0:T(8,128)(2,1)S(1)} %collective-permute-done.8.refs_1_, bf16[2048,128]{1,0:T(8,128)(2,1)S(1)} %collective-permute-done.12.refs_2_, ...), custom_call_target="tpu_custom_call" | custom-call | flops 1 | bytes 1 | tf_op jit(solution)/shard_map/pallas_call | solution.py:111
  45.1 5.7 %collective-permute-done.9.refs_6_ = bf16[64,3584]{1,0:T(8,128)(2,1)} collective-permute-done((bf16[64,3584]{1,0:T(8,128)(2,1)}, bf16[64,3584]{1,0:T(8,128)(2,1)}, u32[]{:S(2)}, u32[]{:S(2)}) %collective-permute-start.9) | collective-permute-done | bytes 458784 | tf_op jit(solution)/shard_map/ppermute | solution.py:23
  52.4 5.8 %all-to-all-start = ((bf16[8,128,512]{2,1,0:T(8,128)(2,1)}), bf16[8,128,512]{2,1,0:T(8,128)(2,1)}, u32[]{:S(2)}, u32[]{:S(2)}) async-start(bf16[8,128,512]{2,1,0:T(8,128)(2,1)} %shard_map.55), calls=%async_computation | async-start | bytes 2097152 | tf_op jit(solution)/shard_map/all_to_all | solution.py:40
  58.2 2.0 %collective-permute-start.14 = (bf16[64,3584]{1,0:T(8,128)(2,1)}, bf16[64,3584]{1,0:T(8,128)(2,1)}, u32[]{:S(2)}, u32[]{:S(2)}) collective-permute-start(bf16[64,3584]{1,0:T(8,128)(2,1)} %collective-permute-done.9.refs_6_), channel_id=1, source_target_pairs={{0,16},{8,24},{16,32},{24,40},{32,48},{40,56},{48,64},{56,72},{64,... | collective-permute-start | bytes 1376264 | tf_op jit(solution)/shard_map/ppermute | solution.py:23
  63.1 1.9 %collective-permute-start.17 = (bf16[64,3584]{1,0:T(8,128)(2,1)}, bf16[64,3584]{1,0:T(8,128)(2,1)}, u32[]{:S(2)}, u32[]{:S(2)}) collective-permute-start(bf16[64,3584]{1,0:T(8,128)(2,1)} %copy-done.4), channel_id=1, source_target_pairs={{0,8},{8,0},{16,24},{24,16},{32,40},{40,32},{48,56},{56,48},{64,72... | collective-permute-start | bytes 1376264 | tf_op jit(solution)/shard_map/ppermute | solution.py:27
  66.6 7.0 %shard_map.56 = (f32[256,896]{1,0:T(8,128)S(1)}, f32[256,896]{1,0:T(8,128)S(1)}) custom-call(s32[1]{0:T(128)} %bitcast.2.core_ref, bf16[64,3584]{1,0:T(8,128)(2,1)S(1)} %copy-done.1, bf16[64,3584]{1,0:T(8,128)(2,1)S(1)} %copy-done.5, bf16[64,3584]{1,0:T(8,128)(2,1)} %collective-permute-done.7.refs_2_, bf16[64,3584]{1,0:T(8,128)(2,1)} %collective-permute-done.10.refs_3_, ...), custom_call_target="tpu_custom_call" | custom-call | flops 1 | bytes 1 | tf_op jit(solution)/shard_map/pallas_call | solution.py:73
  74.6 18.6 %collective-permute-done.14.refs_0_ = bf16[64,3584]{1,0:T(8,128)(2,1)} collective-permute-done((bf16[64,3584]{1,0:T(8,128)(2,1)}, bf16[64,3584]{1,0:T(8,128)(2,1)}, u32[]{:S(2)}, u32[]{:S(2)}) %collective-permute-start.14) | collective-permute-done | bytes 458784 | tf_op jit(solution)/shard_map/ppermute | solution.py:23
  94.9 3.0 %collective-permute-start.19 = (bf16[64,3584]{1,0:T(8,128)(2,1)}, bf16[64,3584]{1,0:T(8,128)(2,1)S(1)}, u32[]{:S(2)}, u32[]{:S(2)}) collective-permute-start(bf16[64,3584]{1,0:T(8,128)(2,1)} %collective-permute-done.15.refs_5_), channel_id=1, source_target_pairs={{0,112},{8,120},{16,0},{24,8},{32,16},{40,24},{48,32},{56,40},{64,... | collective-permute-start | bytes 1376264 | tf_op jit(solution)/shard_map/ppermute | solution.py:23
  100.6 5.7 %collective-permute-done.20.refs_4_ = bf16[64,3584]{1,0:T(8,128)(2,1)S(1)} collective-permute-done((bf16[64,3584]{1,0:T(8,128)(2,1)S(1)}, bf16[64,3584]{1,0:T(8,128)(2,1)S(1)}, u32[]{:S(2)}, u32[]{:S(2)}) %collective-permute-start.20) | collective-permute-done | bytes 458784 | tf_op jit(solution)/shard_map/ppermute | solution.py:27
  108.9 7.1 %all-to-all-start.1 = ((bf16[16,128,512]{2,1,0:T(8,128)(2,1)}), bf16[16,128,512]{2,1,0:T(8,128)(2,1)S(1)}, u32[]{:S(2)}, u32[]{:S(2)}) async-start(bf16[16,128,512]{2,1,0:T(8,128)(2,1)} %broadcast_in_dim.21), calls=%async_computation.1 | async-start | bytes 4194304 | tf_op jit(solution)/shard_map/all_to_all | solution.py:268
  118.2 7.0 %shard_map.59 = (f32[256,896]{1,0:T(8,128)S(1)}, f32[256,896]{1,0:T(8,128)S(1)}) custom-call(s32[1]{0:T(128)} %bitcast.2.core_ref, bf16[64,3584]{1,0:T(8,128)(2,1)} %collective-permute-done.14.refs_0_, bf16[64,3584]{1,0:T(8,128)(2,1)} %collective-permute-done.17.refs_1_, bf16[64,3584]{1,0:T(8,128)(2,1)} %collective-permute-done.21.refs_2_, ...), custom_call_target="tpu_custom_call" | custom-call | flops 1 | bytes 1 | tf_op jit(solution)/shard_map/pallas_call | solution.py:73
  127.1 2.1 %collective-permute-start.24 = (f32[64,896]{1,0:T(8,128)S(1)}, f32[64,896]{1,0:T(8,128)S(1)}, u32[]{:S(2)}, u32[]{:S(2)}) collective-permute-start(f32[64,896]{1,0:T(8,128)S(1)} %get-tuple-element.84), channel_id=1, source_target_pairs={{0,4},{1,5},{2,6},{3,7},{4,0},{5,1},{6,2},{7,3},{8,12},{9,13},{10,... | collective-permute-start | bytes 688136 | tf_op jit(solution)/shard_map/ppermute | solution.py:32
  131.4 2.7 %collective-permute-start.32 = (f32[64,896]{1,0:T(8,128)S(1)}, f32[64,896]{1,0:T(8,128)S(1)}, u32[]{:S(2)}, u32[]{:S(2)}) collective-permute-start(f32[64,896]{1,0:T(8,128)S(1)} %get-tuple-element.97), channel_id=1, source_target_pairs={{0,4},{1,5},{2,6},{3,7},{4,0},{5,1},{6,2},{7,3},{8,12},{9,13},{10,... | collective-permute-start | bytes 688136 | tf_op jit(solution)/shard_map/ppermute | solution.py:32
  134.0 3.2 %collective-permute-done.23 = f32[64,896]{1,0:T(8,128)S(1)} collective-permute-done((f32[64,896]{1,0:T(8,128)S(1)}, f32[64,896]{1,0:T(8,128)S(1)}, u32[]{:S(2)}, u32[]{:S(2)}) %collective-permute-start.23) | collective-permute-done | bytes 229408 | tf_op jit(solution)/shard_map/ppermute | solution.py:32
  137.2 3.9 %collective-permute-start.33 = (f32[64,896]{1,0:T(8,128)S(1)}, f32[64,896]{1,0:T(8,128)S(1)}, u32[]{:S(2)}, u32[]{:S(2)}) collective-permute-start(f32[64,896]{1,0:T(8,128)S(1)} %get-tuple-element.98), channel_id=1, source_target_pairs={{0,6},{1,7},{2,0},{3,1},{4,2},{5,3},{6,4},{7,5},{8,14},{9,15},{10,... | collective-permute-start | bytes 688136 | tf_op jit(solution)/shard_map/ppermute | solution.py:32
  142.8 2.1 %collective-permute-start.27 = (bf16[64,896]{1,0:T(8,128)(2,1)S(1)}, bf16[64,896]{1,0:T(8,128)(2,1)S(1)}, u32[]{:S(2)}, u32[]{:S(2)}) collective-permute-start(bf16[64,896]{1,0:T(8,128)(2,1)S(1)} %add_convert_fusion.1.refs_0_), channel_id=1, source_target_pairs={{0,4},{1,5},{2,6},{3,7},{4,0},{5,1},{6,2},{7,3},{8,12},{9,13},{10,... | collective-permute-start | bytes 344072 | tf_op jit(solution)/shard_map/ppermute | solution.py:32
  144.8 2.1 %collective-permute-start.26 = (bf16[64,896]{1,0:T(8,128)(2,1)S(1)}, bf16[64,896]{1,0:T(8,128)(2,1)S(1)}, u32[]{:S(2)}, u32[]{:S(2)}) collective-permute-start(bf16[64,896]{1,0:T(8,128)(2,1)S(1)} %add_convert_fusion.1.refs_0_), channel_id=1, source_target_pairs={{0,6},{1,7},{2,0},{3,1},{4,2},{5,3},{6,4},{7,5},{8,14},{9,15},{10,... | collective-permute-start | bytes 344072 | tf_op jit(solution)/shard_map/ppermute | solution.py:32
  147.0 4.9 %collective-permute-done.33 = f32[64,896]{1,0:T(8,128)S(1)} collective-permute-done((f32[64,896]{1,0:T(8,128)S(1)}, f32[64,896]{1,0:T(8,128)S(1)}, u32[]{:S(2)}, u32[]{:S(2)}) %collective-permute-start.33) | collective-permute-done | bytes 229408 | tf_op jit(solution)/shard_map/ppermute | solution.py:32
  152.6 2.1 %collective-permute-start.35 = (bf16[64,896]{1,0:T(8,128)(2,1)S(1)}, bf16[64,896]{1,0:T(8,128)(2,1)S(1)}, u32[]{:S(2)}, u32[]{:S(2)}) collective-permute-start(bf16[64,896]{1,0:T(8,128)(2,1)S(1)} %add_convert_fusion.refs_0_), channel_id=1, source_target_pairs={{0,4},{1,5},{2,6},{3,7},{4,0},{5,1},{6,2},{7,3},{8,12},{9,13},{10,... | collective-permute-start | bytes 344072 | tf_op jit(solution)/shard_map/ppermute | solution.py:32
  154.7 2.3 %collective-permute-start.34 = (bf16[64,896]{1,0:T(8,128)(2,1)S(1)}, bf16[64,896]{1,0:T(8,128)(2,1)S(1)}, u32[]{:S(2)}, u32[]{:S(2)}) collective-permute-start(bf16[64,896]{1,0:T(8,128)(2,1)S(1)} %add_convert_fusion.refs_0_), channel_id=1, source_target_pairs={{0,6},{1,7},{2,0},{3,1},{4,2},{5,3},{6,4},{7,5},{8,14},{9,15},{10,... | collective-permute-start | bytes 344072 | tf_op jit(solution)/shard_map/ppermute | solution.py:32
  157.1 2.6 %collective-permute-done.35.refs_2_ = bf16[64,896]{1,0:T(8,128)(2,1)S(1)} collective-permute-done((bf16[64,896]{1,0:T(8,128)(2,1)S(1)}, bf16[64,896]{1,0:T(8,128)(2,1)S(1)}, u32[]{:S(2)}, u32[]{:S(2)}) %collective-permute-start.35) | collective-permute-done | bytes 114720 | tf_op jit(solution)/shard_map/ppermute | solution.py:32
  163.0 3.7 %all-to-all-done.1 = bf16[16,128,512]{2,1,0:T(8,128)(2,1)S(1)} async-done(((bf16[16,128,512]{2,1,0:T(8,128)(2,1)}), bf16[16,128,512]{2,1,0:T(8,128)(2,1)S(1)}, u32[]{:S(2)}, u32[]{:S(2)}) %all-to-all-start.1) | async-done | bytes 2097184 | tf_op jit(solution)/shard_map/all_to_all | solution.py:268
  166.7 6.7 %shard_map.62 = f32[1024,896]{1,0:T(8,128)} custom-call(s32[3]{0:T(128)S(1)} %pad_add_fusion.place_ref, f32[1]{0:T(128)} %bitcast.4.scale_ref, bf16[8,2,128,512]{3,2,1,0:T(8,128)(2,1)S(1)} %bitcast.7, bf16[256,896]{1,0:T(8,128)(2,1)S(1)} %shard_map.58.refs_1_, bf16[256,896]{1,0:T(8,128)(2,1)S(1)} %collective-permute-done.29.refs_2_, ...), custom_call_target="tpu_custom_call" | custom-call | flops 1 | bytes 1 | tf_op jit(solution)/shard_map/pallas_call | solution.py:200
  (95 shorter events, 34.0 us)
Async XLA Ops:
  1.2 22.0 %collective-permute-start.2 = (bf16[512,512]{1,0:T(8,128)(2,1)S(1)}, bf16[512,512]{1,0:T(8,128)(2,1)S(1)}, u32[]{:S(2)}, u32[]{:S(2)}) collective-permute-start(bf16[512,512]{1,0:T(8,128)(2,1)S(1)} %constant_dynamic-slice_fusion), channel_id=1, source_target_pairs={{0,8},{8,0},{16,24},{24,16},{32,40},{40,32},{48,56},{56,48},{64,72... | collective-permute-start | bytes 1572872 | tf_op jit(solution)/shard_map/ppermute | solution.py:27
  4.3 18.9 %collective-permute-start = (bf16[64,3584]{1,0:T(8,128)(2,1)}, bf16[64,3584]{1,0:T(8,128)(2,1)S(1)}, u32[]{:S(2)}, u32[]{:S(2)}) collective-permute-start(bf16[64,3584]{1,0:T(8,128)(2,1)} %refs_0_), channel_id=1, source_target_pairs={{0,16},{8,24},{16,32},{24,40},{32,48},{40,56},{48,64},{56,72},{64,... | collective-permute-start | bytes 1376264 | tf_op jit(solution)/shard_map/ppermute | solution.py:23
  6.2 17.0 %collective-permute-start.1 = (bf16[64,3584]{1,0:T(8,128)(2,1)}, bf16[64,3584]{1,0:T(8,128)(2,1)S(1)}, u32[]{:S(2)}, u32[]{:S(2)}) collective-permute-start(bf16[64,3584]{1,0:T(8,128)(2,1)} %refs_0_), channel_id=1, source_target_pairs={{0,112},{8,120},{16,0},{24,8},{32,16},{40,24},{48,32},{56,40},{64,... | collective-permute-start | bytes 1376264 | tf_op jit(solution)/shard_map/ppermute | solution.py:23
  10.1 7.8 %collective-permute-start.4 = (bf16[512,128]{1,0:T(8,128)(2,1)}, bf16[512,128]{1,0:T(8,128)(2,1)S(1)}, u32[]{:S(2)}, u32[]{:S(2)}) collective-permute-start(bf16[512,128]{1,0:T(8,128)(2,1)} %param.6), channel_id=1, source_target_pairs={{0,4},{1,5},{2,6},{3,7},{4,0},{5,1},{6,2},{7,3},{8,12},{9,13},{10,... | collective-permute-start | bytes 393224 | tf_op jit(solution)/shard_map/ppermute | solution.py:32
  12.4 6.9 %collective-permute-start.3 = (bf16[512,128]{1,0:T(8,128)(2,1)}, bf16[512,128]{1,0:T(8,128)(2,1)S(1)}, u32[]{:S(2)}, u32[]{:S(2)}) collective-permute-start(bf16[512,128]{1,0:T(8,128)(2,1)} %param.6), channel_id=1, source_target_pairs={{0,6},{1,7},{2,0},{3,1},{4,2},{5,3},{6,4},{7,5},{8,14},{9,15},{10,... | collective-permute-start | bytes 393224 | tf_op jit(solution)/shard_map/ppermute | solution.py:32
  24.3 11.8 %collective-permute-start.8 = (bf16[2048,128]{1,0:T(8,128)(2,1)S(1)}, bf16[2048,128]{1,0:T(8,128)(2,1)S(1)}, u32[]{:S(2)}, u32[]{:S(2)}) collective-permute-start(bf16[2048,128]{1,0:T(8,128)(2,1)S(1)} %constant_dynamic-update-slice_fusion.refs_0_), channel_id=1, source_target_pairs={{0,8},{8,0},{16,24},{24,16},{32,40},{40,32},{48,56},{56,48},{64,72... | collective-permute-start | bytes 1572872 | tf_op jit(solution)/shard_map/ppermute | solution.py:27
  24.9 10.9 %collective-permute-start.6 = (bf16[64,3584]{1,0:T(8,128)(2,1)S(1)}, bf16[64,3584]{1,0:T(8,128)(2,1)}, u32[]{:S(2)}, u32[]{:S(2)}) collective-permute-start(bf16[64,3584]{1,0:T(8,128)(2,1)S(1)} %collective-permute-done.refs_4_), channel_id=1, source_target_pairs={{0,16},{8,24},{16,32},{24,40},{32,48},{40,56},{48,64},{56,72},{64,... | collective-permute-start | bytes 1376264 | tf_op jit(solution)/shard_map/ppermute | solution.py:23
  24.9 10.9 %collective-permute-start.7 = (bf16[64,3584]{1,0:T(8,128)(2,1)S(1)}, bf16[64,3584]{1,0:T(8,128)(2,1)}, u32[]{:S(2)}, u32[]{:S(2)}) collective-permute-start(bf16[64,3584]{1,0:T(8,128)(2,1)S(1)} %collective-permute-done.1.refs_1_), channel_id=1, source_target_pairs={{0,112},{8,120},{16,0},{24,8},{32,16},{40,24},{48,32},{56,40},{64,... | collective-permute-start | bytes 1376264 | tf_op jit(solution)/shard_map/ppermute | solution.py:23
  36.7 14.0 %collective-permute-start.9 = (bf16[64,3584]{1,0:T(8,128)(2,1)}, bf16[64,3584]{1,0:T(8,128)(2,1)}, u32[]{:S(2)}, u32[]{:S(2)}) collective-permute-start(bf16[64,3584]{1,0:T(8,128)(2,1)} %collective-permute-done.6.refs_5_), channel_id=1, source_target_pairs={{0,16},{8,24},{16,32},{24,40},{32,48},{40,56},{48,64},{56,72},{64,... | collective-permute-start | bytes 1376264 | tf_op jit(solution)/shard_map/ppermute | solution.py:23
  37.1 14.1 %collective-permute-start.11 = (bf16[64,3584]{1,0:T(8,128)(2,1)}, bf16[64,3584]{1,0:T(8,128)(2,1)}, u32[]{:S(2)}, u32[]{:S(2)}) collective-permute-start(bf16[64,3584]{1,0:T(8,128)(2,1)} %collective-permute-done.7.refs_2_), channel_id=1, source_target_pairs={{0,8},{8,0},{16,24},{24,16},{32,40},{40,32},{48,56},{56,48},{64,72... | collective-permute-start | bytes 1376264 | tf_op jit(solution)/shard_map/ppermute | solution.py:27
  40.1 12.3 %collective-permute-start.10 = (bf16[64,3584]{1,0:T(8,128)(2,1)}, bf16[64,3584]{1,0:T(8,128)(2,1)}, u32[]{:S(2)}, u32[]{:S(2)}) collective-permute-start(bf16[64,3584]{1,0:T(8,128)(2,1)} %collective-permute-done.7.refs_2_), channel_id=1, source_target_pairs={{0,112},{8,120},{16,0},{24,8},{32,16},{40,24},{48,32},{56,40},{64,... | collective-permute-start | bytes 1376264 | tf_op jit(solution)/shard_map/ppermute | solution.py:23
  52.4 46.6 %all-to-all-start = ((bf16[8,128,512]{2,1,0:T(8,128)(2,1)}), bf16[8,128,512]{2,1,0:T(8,128)(2,1)}, u32[]{:S(2)}, u32[]{:S(2)}) async-start(bf16[8,128,512]{2,1,0:T(8,128)(2,1)} %shard_map.55), calls=%async_computation | async-start | bytes 2097152 | tf_op jit(solution)/shard_map/all_to_all | solution.py:40
  58.2 35.0 %collective-permute-start.14 = (bf16[64,3584]{1,0:T(8,128)(2,1)}, bf16[64,3584]{1,0:T(8,128)(2,1)}, u32[]{:S(2)}, u32[]{:S(2)}) collective-permute-start(bf16[64,3584]{1,0:T(8,128)(2,1)} %collective-permute-done.9.refs_6_), channel_id=1, source_target_pairs={{0,16},{8,24},{16,32},{24,40},{32,48},{40,56},{48,64},{56,72},{64,... | collective-permute-start | bytes 1376264 | tf_op jit(solution)/shard_map/ppermute | solution.py:23
  60.3 33.0 %collective-permute-start.15 = (bf16[64,3584]{1,0:T(8,128)(2,1)}, bf16[64,3584]{1,0:T(8,128)(2,1)}, u32[]{:S(2)}, u32[]{:S(2)}) collective-permute-start(bf16[64,3584]{1,0:T(8,128)(2,1)} %collective-permute-done.11.refs_7_), channel_id=1, source_target_pairs={{0,112},{8,120},{16,0},{24,8},{32,16},{40,24},{48,32},{56,40},{64,... | collective-permute-start | bytes 1376264 | tf_op jit(solution)/shard_map/ppermute | solution.py:23
  61.5 31.7 %collective-permute-start.16 = (bf16[64,3584]{1,0:T(8,128)(2,1)}, bf16[64,3584]{1,0:T(8,128)(2,1)}, u32[]{:S(2)}, u32[]{:S(2)}) collective-permute-start(bf16[64,3584]{1,0:T(8,128)(2,1)} %collective-permute-done.6.refs_5_), channel_id=1, source_target_pairs={{0,8},{8,0},{16,24},{24,16},{32,40},{40,32},{48,56},{56,48},{64,72... | collective-permute-start | bytes 1376264 | tf_op jit(solution)/shard_map/ppermute | solution.py:27
  63.1 30.1 %collective-permute-start.17 = (bf16[64,3584]{1,0:T(8,128)(2,1)}, bf16[64,3584]{1,0:T(8,128)(2,1)}, u32[]{:S(2)}, u32[]{:S(2)}) collective-permute-start(bf16[64,3584]{1,0:T(8,128)(2,1)} %copy-done.4), channel_id=1, source_target_pairs={{0,8},{8,0},{16,24},{24,16},{32,40},{40,32},{48,56},{56,48},{64,72... | collective-permute-start | bytes 1376264 | tf_op jit(solution)/shard_map/ppermute | solution.py:27
  65.1 35.5 %collective-permute-start.21 = (bf16[64,3584]{1,0:T(8,128)(2,1)S(1)}, bf16[64,3584]{1,0:T(8,128)(2,1)}, u32[]{:S(2)}, u32[]{:S(2)}) collective-permute-start(bf16[64,3584]{1,0:T(8,128)(2,1)S(1)} %copy-done.1), channel_id=1, source_target_pairs={{0,8},{8,0},{16,24},{24,16},{32,40},{40,32},{48,56},{56,48},{64,72... | collective-permute-start | bytes 1376264 | tf_op jit(solution)/shard_map/ppermute | solution.py:27
  93.2 13.1 %collective-permute-start.20 = (bf16[64,3584]{1,0:T(8,128)(2,1)S(1)}, bf16[64,3584]{1,0:T(8,128)(2,1)S(1)}, u32[]{:S(2)}, u32[]{:S(2)}) collective-permute-start(bf16[64,3584]{1,0:T(8,128)(2,1)S(1)} %copy-done.3), channel_id=1, source_target_pairs={{0,8},{8,0},{16,24},{24,16},{32,40},{40,32},{48,56},{56,48},{64,72... | collective-permute-start | bytes 1376264 | tf_op jit(solution)/shard_map/ppermute | solution.py:27
  94.7 12.6 %collective-permute-start.18 = (bf16[64,3584]{1,0:T(8,128)(2,1)}, bf16[64,3584]{1,0:T(8,128)(2,1)S(1)}, u32[]{:S(2)}, u32[]{:S(2)}) collective-permute-start(bf16[64,3584]{1,0:T(8,128)(2,1)} %collective-permute-done.16.refs_3_), channel_id=1, source_target_pairs={{0,16},{8,24},{16,32},{24,40},{32,48},{40,56},{48,64},{56,72},{64,... | collective-permute-start | bytes 1376264 | tf_op jit(solution)/shard_map/ppermute | solution.py:23
  94.9 12.4 %collective-permute-start.19 = (bf16[64,3584]{1,0:T(8,128)(2,1)}, bf16[64,3584]{1,0:T(8,128)(2,1)S(1)}, u32[]{:S(2)}, u32[]{:S(2)}) collective-permute-start(bf16[64,3584]{1,0:T(8,128)(2,1)} %collective-permute-done.15.refs_5_), channel_id=1, source_target_pairs={{0,112},{8,120},{16,0},{24,8},{32,16},{40,24},{48,32},{56,40},{64,... | collective-permute-start | bytes 1376264 | tf_op jit(solution)/shard_map/ppermute | solution.py:23
  108.9 57.7 %all-to-all-start.1 = ((bf16[16,128,512]{2,1,0:T(8,128)(2,1)}), bf16[16,128,512]{2,1,0:T(8,128)(2,1)S(1)}, u32[]{:S(2)}, u32[]{:S(2)}) async-start(bf16[16,128,512]{2,1,0:T(8,128)(2,1)} %broadcast_in_dim.21), calls=%async_computation.1 | async-start | bytes 4194304 | tf_op jit(solution)/shard_map/all_to_all | solution.py:268
  116.0 9.7 %collective-permute-start.22 = (f32[256,896]{1,0:T(8,128)}, f32[256,896]{1,0:T(8,128)S(1)}, u32[]{:S(2)}, u32[]{:S(2)}) collective-permute-start(f32[256,896]{1,0:T(8,128)} %copy-done.10), channel_id=1, source_target_pairs={{0,1},{1,0},{2,3},{3,2},{4,5},{5,4},{6,7},{7,6},{8,9},{9,8},{10,11... | collective-permute-start | bytes 2752520 | tf_op jit(solution)/shard_map/ppermute | solution.py:36
  125.8 11.4 %collective-permute-start.23 = (f32[64,896]{1,0:T(8,128)S(1)}, f32[64,896]{1,0:T(8,128)S(1)}, u32[]{:S(2)}, u32[]{:S(2)}) collective-permute-start(f32[64,896]{1,0:T(8,128)S(1)} %get-tuple-element.83), channel_id=1, source_target_pairs={{0,2},{1,3},{2,4},{3,5},{4,6},{5,7},{6,0},{7,1},{8,10},{9,11},{10,... | collective-permute-start | bytes 688136 | tf_op jit(solution)/shard_map/ppermute | solution.py:32
  127.1 14.0 %collective-permute-start.24 = (f32[64,896]{1,0:T(8,128)S(1)}, f32[64,896]{1,0:T(8,128)S(1)}, u32[]{:S(2)}, u32[]{:S(2)}) collective-permute-start(f32[64,896]{1,0:T(8,128)S(1)} %get-tuple-element.84), channel_id=1, source_target_pairs={{0,4},{1,5},{2,6},{3,7},{4,0},{5,1},{6,2},{7,3},{8,12},{9,13},{10,... | collective-permute-start | bytes 688136 | tf_op jit(solution)/shard_map/ppermute | solution.py:32
  129.2 13.0 %collective-permute-start.25 = (f32[64,896]{1,0:T(8,128)S(1)}, f32[64,896]{1,0:T(8,128)S(1)}, u32[]{:S(2)}, u32[]{:S(2)}) collective-permute-start(f32[64,896]{1,0:T(8,128)S(1)} %get-tuple-element.85), channel_id=1, source_target_pairs={{0,6},{1,7},{2,0},{3,1},{4,2},{5,3},{6,4},{7,5},{8,14},{9,15},{10,... | collective-permute-start | bytes 688136 | tf_op jit(solution)/shard_map/ppermute | solution.py:32
  130.8 14.0 %collective-permute-start.31 = (f32[64,896]{1,0:T(8,128)S(1)}, f32[64,896]{1,0:T(8,128)S(1)}, u32[]{:S(2)}, u32[]{:S(2)}) collective-permute-start(f32[64,896]{1,0:T(8,128)S(1)} %get-tuple-element.96), channel_id=1, source_target_pairs={{0,2},{1,3},{2,4},{3,5},{4,6},{5,7},{6,0},{7,1},{8,10},{9,11},{10,... | collective-permute-start | bytes 688136 | tf_op jit(solution)/shard_map/ppermute | solution.py:32
  131.4 15.6 %collective-permute-start.32 = (f32[64,896]{1,0:T(8,128)S(1)}, f32[64,896]{1,0:T(8,128)S(1)}, u32[]{:S(2)}, u32[]{:S(2)}) collective-permute-start(f32[64,896]{1,0:T(8,128)S(1)} %get-tuple-element.97), channel_id=1, source_target_pairs={{0,4},{1,5},{2,6},{3,7},{4,0},{5,1},{6,2},{7,3},{8,12},{9,13},{10,... | collective-permute-start | bytes 688136 | tf_op jit(solution)/shard_map/ppermute | solution.py:32
  137.2 14.7 %collective-permute-start.33 = (f32[64,896]{1,0:T(8,128)S(1)}, f32[64,896]{1,0:T(8,128)S(1)}, u32[]{:S(2)}, u32[]{:S(2)}) collective-permute-start(f32[64,896]{1,0:T(8,128)S(1)} %get-tuple-element.98), channel_id=1, source_target_pairs={{0,6},{1,7},{2,0},{3,1},{4,2},{5,3},{6,4},{7,5},{8,14},{9,15},{10,... | collective-permute-start | bytes 688136 | tf_op jit(solution)/shard_map/ppermute | solution.py:32
  142.2 12.5 %collective-permute-start.28 = (bf16[64,896]{1,0:T(8,128)(2,1)S(1)}, bf16[64,896]{1,0:T(8,128)(2,1)S(1)}, u32[]{:S(2)}, u32[]{:S(2)}) collective-permute-start(bf16[64,896]{1,0:T(8,128)(2,1)S(1)} %add_convert_fusion.1.refs_0_), channel_id=1, source_target_pairs={{0,2},{1,3},{2,4},{3,5},{4,6},{5,7},{6,0},{7,1},{8,10},{9,11},{10,... | collective-permute-start | bytes 344072 | tf_op jit(solution)/shard_map/ppermute | solution.py:32
  142.8 14.2 %collective-permute-start.27 = (bf16[64,896]{1,0:T(8,128)(2,1)S(1)}, bf16[64,896]{1,0:T(8,128)(2,1)S(1)}, u32[]{:S(2)}, u32[]{:S(2)}) collective-permute-start(bf16[64,896]{1,0:T(8,128)(2,1)S(1)} %add_convert_fusion.1.refs_0_), channel_id=1, source_target_pairs={{0,4},{1,5},{2,6},{3,7},{4,0},{5,1},{6,2},{7,3},{8,12},{9,13},{10,... | collective-permute-start | bytes 344072 | tf_op jit(solution)/shard_map/ppermute | solution.py:32
  144.8 12.2 %collective-permute-start.26 = (bf16[64,896]{1,0:T(8,128)(2,1)S(1)}, bf16[64,896]{1,0:T(8,128)(2,1)S(1)}, u32[]{:S(2)}, u32[]{:S(2)}) collective-permute-start(bf16[64,896]{1,0:T(8,128)(2,1)S(1)} %add_convert_fusion.1.refs_0_), channel_id=1, source_target_pairs={{0,6},{1,7},{2,0},{3,1},{4,2},{5,3},{6,4},{7,5},{8,14},{9,15},{10,... | collective-permute-start | bytes 344072 | tf_op jit(solution)/shard_map/ppermute | solution.py:32
  152.6 7.1 %collective-permute-start.35 = (bf16[64,896]{1,0:T(8,128)(2,1)S(1)}, bf16[64,896]{1,0:T(8,128)(2,1)S(1)}, u32[]{:S(2)}, u32[]{:S(2)}) collective-permute-start(bf16[64,896]{1,0:T(8,128)(2,1)S(1)} %add_convert_fusion.refs_0_), channel_id=1, source_target_pairs={{0,4},{1,5},{2,6},{3,7},{4,0},{5,1},{6,2},{7,3},{8,12},{9,13},{10,... | collective-permute-start | bytes 344072 | tf_op jit(solution)/shard_map/ppermute | solution.py:32
  (20 other events, 210.9 us)
